TPU v7x, 256 devices: a whole 4x4x8 slice. The times are simulated.
256 devices in a mesh: group: 4 (over z_lo, core), fsdp: 64 (over y, z_hi, x).
Axes of the slice: x: 4, y: 4, z: 8 (z_hi: 4, z_lo: 2; z = z_hi * 2 + z_lo), core: 2. Of those that a mesh axis runs over, the one named last changes fastest.
Arguments:
- head_out: bfloat16 [4, 24576, 2048], P('group', 'fsdp'), may hold values from -6 to 6
- gate_in: bfloat16 [4, 24576, 2048], P('group', 'fsdp'), may hold values from -8 to 8
- cotangent: bfloat16 [4, 24576, 2048], P('group', 'fsdp'), may hold values from -6 to 6
- momentum: float32 [4, 2048, 2048], P('group', 'fsdp'), may hold values from -6 to 6
- chosen_index: int32 [4, 2048, 512], P('group', 'fsdp'), may hold values from 0 to 63, as said below
- out_weight: bfloat16 [2048, 2048], P('fsdp'), may hold values from -0.125 to 0.125
- norm_gain: float32 [128], replicated, may hold values from 0.1 to 1.9
Outputs:
- head_grad: bfloat16 [4, 24576, 2048], P('group', 'fsdp')
- gate_grad: bfloat16 [4, 24576, 2048], P('group', 'fsdp')
- new_momentum: float32 [4, 2048, 2048], P('group', 'fsdp')
- update: float32 [2048, 2048], P('fsdp')
Inputs may be any that keep to these rules, and one draw needn't show every extreme that they name: `chosen_index`: within each transform block, the 16 entries of a group are distinct.
All inputs are finite; a program needn't handle non-finite values.
Results may differ from a plain program's by a relative error of at most 0.0022.
Values may be sent and summed in bfloat16 or wider, within the bound.
A program may use at most 128 MiB of HBM per device.

v0:
```python
import jax
import jax.numpy as jnp
from jax import lax
from jax.sharding import PartitionSpec as P

SPAN = 64
KEEP = 16


epsilon = 1e-06
decay_rate = 0.999


def cosine_table(width):
    freq = jnp.arange(width, dtype=jnp.float32)[:, None]
    place = jnp.arange(width, dtype=jnp.float32)[None, :]
    scale = jnp.where(freq == 0, jnp.sqrt(1.0 / width), jnp.sqrt(2.0 / width))
    return jnp.cos(jnp.pi * (place + 0.5) * freq / width) * scale


def gated_output(heads, gates, norm_gain):
    row_total = heads.shape[0]
    per_head = heads.reshape(row_total, -1, norm_gain.shape[0])
    scaled = per_head * lax.rsqrt(jnp.mean(per_head * per_head, axis=-1, keepdims=True) + epsilon)
    normed = (scaled * norm_gain).reshape(row_total, -1)
    return normed * jax.nn.silu(gates)


def pick_table(where):
    return (where[..., None] == jnp.arange(SPAN, dtype=jnp.int32)).astype(jnp.float32)


def local(head_out, gate_in, cotangent, momentum, chosen_index, out_weight, norm_gain):
    highest = lax.Precision.HIGHEST
    heads = head_out[0].astype(jnp.float32)
    gates = gate_in[0].astype(jnp.float32)
    upstream_in = cotangent[0]
    gated, pullback = jax.vjp(lambda a, b: gated_output(a, b, norm_gain), heads, gates)
    gated_low = gated.astype(jnp.bfloat16)
    upstream = jnp.einsum(
        "tm,km->tk",
        upstream_in,
        lax.all_gather(out_weight, "fsdp", axis=0, tiled=True),
        preferred_element_type=jnp.float32,
    )
    head_grad, gate_grad = pullback(upstream)
    local_rows = momentum.shape[1]
    width = momentum.shape[2]
    token_total = upstream_in.shape[0] * lax.axis_size("fsdp")
    contract = (((0,), (0,)), ((), ()))
    whole = lax.dot_general(gated_low, upstream_in, contract, preferred_element_type=jnp.float32)
    summed = lax.psum_scatter(whole, "fsdp", scatter_dimension=0, tiled=True)
    gradient = summed * token_total ** (-0.5)
    moment = decay_rate * momentum[0] + gradient
    block_count = width // SPAN
    cosine = cosine_table(SPAN)
    blocked = moment.reshape(local_rows, block_count, SPAN)
    coeffs = jnp.einsum("rck,fk->rcf", blocked, cosine, precision=highest)
    onehot = pick_table(chosen_index[0].reshape(local_rows, block_count, KEEP))
    kept = jnp.einsum("rcf,rcjf->rcj", coeffs, onehot, precision=highest)
    own = jnp.einsum("rcj,rcjf->rcf", kept, onehot, precision=highest)
    new_moment = moment - jnp.einsum("rcf,fk->rck", own, cosine, precision=highest).reshape(
        local_rows, width
    )
    every_kept, every_where = (
        lax.all_gather(kept.reshape(1, local_rows, -1), "group", axis=0, tiled=True),
        lax.all_gather(chosen_index, "group", axis=0, tiled=True),
    )
    members = every_kept.shape[0]
    every_kept = every_kept.reshape(members, local_rows, block_count, KEEP)
    every_hot = pick_table(every_where.reshape(members, local_rows, block_count, KEEP))
    dense = jnp.einsum("grcj,grcjf->grcf", every_kept, every_hot, precision=highest)
    decoded = jnp.sum(jnp.einsum("grcf,fk->grck", dense, cosine, precision=highest), axis=0)
    update = (decoded / members).reshape(local_rows, width)
    return (
        head_grad.astype(jnp.bfloat16)[None],
        gate_grad.astype(jnp.bfloat16)[None],
        new_moment[None],
        update,
    )


def solution(mesh):
    placed = (
        P("group", "fsdp", None),
        P("group", "fsdp", None),
        P("group", "fsdp", None),
        P("group", "fsdp", None),
        P("group", "fsdp", None),
        P("fsdp", None),
        P(),
    )
    return jax.shard_map(
        local,
        mesh=mesh,
        in_specs=placed,
        out_specs=(
            P("group", "fsdp", None),
            P("group", "fsdp", None),
            P("group", "fsdp", None),
            P("fsdp", None),
        ),
        check_vma=False,
    )
```

profile of v0, /device:TPU:1, one launch (start us, length us, event | category | flops | bytes accessed | tf_op | source)
XLA Modules:
  0.0 657.0 jit_solution(17616512589572621502)
XLA Ops:
  7.2 0.7 all-gather.2.cloned.1.call-update
  8.0 1.8 convert_bitcast_fusion.1
  9.7 2.4 copy.46
  12.1 0.4 convert_bitcast_fusion.2
  12.5 2.4 copy.50
  14.9 108.1 %all-gather.2.cloned.1.call-done = bf16[2048,2048]{1,0:T(8,128)(2,1)} async-done(((bf16[32,2048]{1,0:T(8,128)(2,1)}), bf16[2048,2048]{1,0:T(8,128)(2,1)}) %all-gather.2.cloned.1.call-update) | async-done | bytes 8388624 | tf_op jit(solution)/shard_map/all_gather | solution.py:43
  123.0 5.9 fusion.31
  128.9 0.8 fusion.52
  129.7 0.8 copy-done.4
  130.5 0.7 copy.48
  131.2 0.2 bitcast_multiply_fusion.1
  131.4 1.7 copy-done.2
  133.1 1.7 multiply_reduce_fusion.1
  134.8 0.7 copy.29
  135.5 1.4 fusion.39
  136.9 0.1 copy.30
  137.1 3.4 fusion.25
  140.5 8.3 %fusion.27 = f32[2048,2048]{1,0:T(8,128)} fusion(bf16[48,8,16,128]{3,2,1,0:T(8,128)(2,1)S(1)} %bitcast.152, bf16[1,384,2048]{2,1,0:T(8,128)(2,1)S(1)} %copy-done), kind=kOutput, calls=%fused_computation.41 | convolution fusion | flops 3221225472 | bytes 19922944 | tf_op jit(solution)/shard_map/dot_general | solution.py:51
  148.8 0.8 copy-done.9
  149.6 0.1 copy.33
  149.7 1.3 copy.34
  151.0 12.9 %all_gather.11 = s32[4,32,512]{2,1,0:T(8,128)S(1)} all-gather(s32[1,32,512]{2,1,0:T(8,128)S(1)} %copy-done.9), channel_id=1, replica_groups=mesh['group'=4,'fsdp'=64] {'group'}, dimensions={0}, use_global_device_ids=true | all-gather | bytes 327680 | tf_op jit(solution)/shard_map/all_gather | solution.py:67
  163.9 0.3 copy.37
  164.2 2.8 copy.38
  167.0 0.1 copy.32
  167.2 0.9 mul.221
  168.0 0.9 broadcast_in_dim.28
  168.9 0.1 copy-done.5
  169.1 0.5 copy-done.6
  169.5 5.2 fusion.33
  174.7 395.4 %reduce-scatter.2.cloned.1.call-done = f32[32,2048]{1,0:T(8,128)} async-done(((f32[2048,2048]{1,0:T(8,128)}), f32[32,2048]{1,0:T(8,128)}) %reduce-scatter.2.cloned.1.call-update) | async-done | bytes 262160 | tf_op jit(solution)/shard_map/reduce_scatter | solution.py:52
  570.1 1.0 bitcast_add_fusion
  571.1 0.2 reshape.134
  571.3 0.7 fusion.37
  572.0 9.1 %fusion.3 = f32[32,32,1,16]{3,2,1,0:T(1,128)S(1)} fusion(f32[32,32,64,1]{2,3,1,0:T(1,128)S(1)} %bitcast.160, s32[32,32,16]{2,1,0:T(8,128)} %copy.34), kind=kOutput, calls=%fused_computation.5 | convolution fusion | flops 13631488 | bytes 393216 | tf_op jit(solution)/shard_map/rcf,rcjf->rcj/dot_general | solution.py:60
  581.1 0.4 copy.40
  581.5 0.4 copy.41
  581.9 5.9 fusion.2
  587.9 0.7 fusion.35
  588.6 0.2 reshape.135
  588.8 0.7 subtract_bitcast_fusion
  589.5 0.1 copy.35
  589.6 31.9 %all_gather.10 = f32[4,32,512]{2,1,0:T(8,128)S(1)} all-gather(f32[1,32,512]{2,1,0:T(8,128)S(1)} %copy.35), channel_id=1, replica_groups=mesh['group'=4,'fsdp'=64] {'group'}, dimensions={0}, use_global_device_ids=true | all-gather | bytes 327680 | tf_op jit(solution)/shard_map/all_gather | solution.py:66
  621.5 0.3 copy.36
  621.9 3.3 copy.43
  625.2 22.1 %fusion = f32[4,32,32,1,64]{4,3,2,1,0:T(1,128)S(1)} fusion(f32[4,32,32,16,1]{3,4,2,1,0:T(1,128)} %copy.43, s32[4,32,32,16]{3,2,1,0:T(8,128)} %copy.38), kind=kOutput, calls=%fused_computation.1 | convolution fusion | flops 54525952 | bytes 1572864 | tf_op jit(solution)/shard_map/grcj,grcjf->grcf/dot_general | solution.py:72
  647.3 1.9 convolution_reduce_fusion
  649.3 0.9 div.52
  (28 shorter events, 0.3 us)
Async XLA Ops:
  7.2 115.8 %copy-start = (bf16[1,384,2048]{2,1,0:T(8,128)(2,1)S(1)}, bf16[1,384,2048]{2,1,0:T(8,128)(2,1)}, u32[]{:S(2)}) copy-start(bf16[1,384,2048]{2,1,0:T(8,128)(2,1)} %param.9) | copy-start | bytes 4718596
  7.2 115.8 %all-gather.2.cloned.1.call-start = ((), (), s32[]{:S(2)}) async-start(), calls=%async_computation.1 | async-start | bytes 8519680 | tf_op jit(solution)/shard_map/all_gather | solution.py:43
  7.9 562.2 %reduce-scatter.2.cloned.1.call-start = ((), (), s32[]{:S(2)}) async-start(), calls=%async_computation.2 | async-start | bytes 17039360 | tf_op jit(solution)/shard_map/reduce_scatter | solution.py:52
  9.7 2.4 copy-start.3
  128.9 1.6 copy-start.4
  130.5 0.7 copy-start.11
  131.2 1.9 copy-start.2
  148.7 0.8 copy-start.9
  149.6 17.4 %copy-start.12 = (f32[128]{0:T(128)S(1)}, f32[128]{0:T(128)}, u32[]{:S(2)}) copy-start(f32[128]{0:T(128)} %param.13) | copy-start | bytes 1540
  149.6 17.5 %copy-start.10 = (f32[384,16]{0,1:T(8,128)S(1)}, f32[384,16]{0,1:T(8,128)}, u32[]{:S(2)}) copy-start(f32[384,16]{0,1:T(8,128)} %get-tuple-element.9) | copy-start | bytes 73732
  167.2 1.9 copy-start.5
  167.2 2.4 copy-start.6
  169.5 400.6 %copy-start.8 = (f32[1,32,2048]{2,1,0:T(8,128)S(1)}, f32[1,32,2048]{2,1,0:T(8,128)}, u32[]{:S(2)}) copy-start(f32[1,32,2048]{2,1,0:T(8,128)} %param.10) | copy-start | bytes 786436
  572.0 9.9 %copy-start.7 = (s32[32,32,16]{2,1,0:T(8,128)S(1)}, s32[32,32,16]{2,1,0:T(8,128)}, u32[]{:S(2)}) copy-start(s32[32,32,16]{2,1,0:T(8,128)} %copy.34) | copy-start | bytes 196612
  625.2 25.0 %copy-start.1 = (bf16[1,384,2048]{2,1,0:T(8,128)(2,1)S(1)}, bf16[1,384,2048]{2,1,0:T(8,128)(2,1)}, u32[]{:S(2)}) copy-start(bf16[1,384,2048]{2,1,0:T(8,128)(2,1)} %param.9) | copy-start | bytes 4718596
Sparse Core Ops, SparseCore 0:
  11.3 111.6 all-gather.1
  148.9 421.1 reduce-scatter.1
where the time goes:
time: 657 us
  waiting for transfers between devices  504 us (77%)
  matrix products  54.6 us (8%)
  blocking collectives  44.8 us (7%)
  local copies, waits for them, and re-layouts  22.3 us (3%)
  other arithmetic  16.6 us (3%)
  between operations  14.3 us (2%)
    reduce_scatter x1, waiting for transfers between devices, local(): summed = lax.psum_scatter(whole, 'fsdp', scatter_dimension=0, tiled=True)  395 us
    all_gather x1, waiting for transfers between devices, local(): lax.all_gather(out_weight, 'fsdp', axis=0, tiled=True)  108 us
    all_gather x1, blocking collectives, local(): lax.all_gather(kept.reshape(1, local_rows, -1), 'group', axis=0, tiled=True)  31.9 us
    dot_general x1, matrix products, local(): jnp.einsum('grcj,grcjf->grcf', every_kept, every_hot, precision=highest)  22.1 us
  transfers between devices with their start and end apart: 2, of which 2 were waited for; matrix products, arithmetic and copies ran while one was open for 3% of the time, Pallas kernels for 0%

commit v1 on v0

v1 whole, which is shorter than its diff:
```python
import functools

import jax
import jax.numpy as jnp
import numpy as np
from jax import lax
from jax.experimental import pallas as pl
from jax.experimental.pallas import tpu as pltpu
from jax.sharding import PartitionSpec as P

MESH = pl.DeviceIdType.MESH
HIGHEST = lax.Precision.HIGHEST
F32 = jnp.float32
BF16 = jnp.bfloat16

SPAN = 64
KEEP = 16
HDIM = 128
TOK = 384
WIDTH = 2048
ROWS = 32
SUB = 512
EPS = 1e-06
DECAY = 0.999

PIECES = ((0, 0), (1, 0), (0, 1), (1, 1))
DOWN_ORDER = (0, 2, 3, 1)


def remote(src, dst, send, recv, device):
    return pltpu.make_async_remote_copy(
        src_ref=src, dst_ref=dst, send_sem=send, recv_sem=recv, device_id=device, device_id_type=MESH
    )


def kernel(
    head_hbm, gate_hbm, cot_hbm, mom_hbm, idx_hbm, w_hbm, gain_ref, dct_ref, idct_ref,
    hgrad_hbm, ggrad_hbm, newmom_hbm, update_hbm,
    heads, gates, cot, mom, idx, w6, low, gsend, gt, cslot, p2s, p2r, q, p3r, dec, dec_r, pair, pair_r,
    newmom, update, perm, spread, upb, hgrad, ggrad,
    load_sem, own_sem, out_sem,
    wx_s, wx_r, wy_s, wy_r, up_s, up_r, dn_s, dn_r, sib_s, sib_r,
    c1_s, c1_r, c2_s, c2_r, gt_s, gt_r, s2_s, s2_r, s3_s, s3_r, d_s, d_r, e_s, e_r,
):
    f = lax.axis_index("fsdp")
    g = lax.axis_index("group")
    y, z, x = f // 16, (f // 4) % 4, f % 4
    lo, core = g // 2, g % 2
    sibling = {"fsdp": f, "group": g + 1 - 2 * core}
    across = {"fsdp": f, "group": (g + 2) % 4}
    above = {"fsdp": y * 16 + ((z + lo) % 4) * 4 + x, "group": (g + 2) % 4}
    below = {"fsdp": y * 16 + ((z + 3 + lo) % 4) * 4 + x, "group": (g + 2) % 4}

    def at_x(d):
        return {"fsdp": y * 16 + z * 4 + (x + d) % 4, "group": g}

    def at_y(d):
        return {"fsdp": ((y + d) % 4) * 16 + z * 4 + x, "group": g}

    def at_z(d):
        return {"fsdp": y * 16 + ((z + d) % 4) * 4 + x, "group": g}

    along = (at_x, at_y)
    mine = (x, y)

    barrier = pltpu.get_barrier_semaphore()
    partners = [at(d) for at in (at_x, at_y, at_z) for d in (1, 2, 3)] + [sibling, above, below]
    for device in partners:
        pl.semaphore_signal(barrier, inc=1, device_id=device, device_id_type=MESH)
    pl.semaphore_wait(barrier, len(partners))

    def wx(d):
        half = w_hbm.at[pl.ds(pl.multiple_of(core * 16, 16), 16)]
        return remote(half, w6.at[y, z, x, core], wx_s.at[d - 1], wx_r.at[d - 1], at_x(d))

    def wy(d):
        part = w6.at[y, z, :, core]
        return remote(part, part, wy_s.at[d - 1], wy_r.at[d - 1], at_y(d))

    def up(p):
        part = w6.at[(y + p % 4) % 4, (z + 8 - p // 4 - 1 + lo) % 4, :, core]
        return remote(part, part, up_s.at[p], up_r.at[p], above)

    def down_piece(p):
        return DOWN_ORDER[p] if p < 4 else p - 2

    def down(p):
        part = w6.at[(y + down_piece(p)) % 4, (z + p // 4 + lo) % 4, :, core]
        return remote(part, part, dn_s.at[p], dn_r.at[p], below)

    def to_sibling(n):
        if n < 4:
            part = w6.at[(y + n) % 4, z, :, core]
        elif n < 10:
            part = w6.at[(y + (n - 4) % 4) % 4, (z + 3 - (n - 4) // 4) % 4, :, core]
        else:
            part = w6.at[(y + down_piece(n - 10)) % 4, (z + 1 + (n - 10) // 4) % 4, :, core]
        return remote(part, part, sib_s.at[n], sib_r.at[n], sibling)

    def first(axis, s, way):
        src = cot_hbm.at[:, pl.ds((axis * 2 + s) * SUB, SUB)]
        dst = cslot.at[axis, s, mine[axis]]
        return remote(src, dst, c1_s.at[axis, s, way], c1_r.at[axis, s, way], along[axis](1 + 2 * way))

    def second(axis, s, way):
        part = cslot.at[axis, s, (mine[axis] + 3 + 2 * way) % 4, pl.ds(way * (TOK // 2), TOK // 2)]
        return remote(part, part, c2_s.at[axis, s, way], c2_r.at[axis, s, way], along[axis](1 + 2 * way))

    def gated_to(axis, d):
        src = gsend.at[axis, (mine[axis] + d) % 4]
        dst = gt.at[axis, :, pl.ds(pl.multiple_of(mine[axis] * TOK, 128), TOK)]
        return remote(src, dst, gt_s.at[axis, d - 1], gt_r.at[axis, d - 1], along[axis](d))

    def own_gated(axis):
        src = gsend.at[axis, mine[axis]]
        dst = gt.at[axis, :, pl.ds(pl.multiple_of(mine[axis] * TOK, 128), TOK)]
        return pltpu.make_async_copy(src, dst, own_sem.at[axis])

    def stage2(n, d):
        return remote(
            p2s.at[n, d - 1], p2r.at[n, d - 1], s2_s.at[n, d - 1], s2_r.at[n, d - 1], along[1 - PIECES[n][0]](d)
        )

    def stage3(n, d):
        src = q.at[n, pl.ds(pl.multiple_of(((z + d) % 4) * ROWS, ROWS), ROWS)]
        return remote(src, p3r.at[n, d - 1], s3_s.at[n, d - 1], s3_r.at[n, d - 1], at_z(d))

    def to_pair(n):
        return remote(dec.at[n], dec_r.at[n], d_s.at[n], d_r.at[n], sibling)

    def to_across(n):
        return remote(pair.at[n], pair_r.at[n], e_s.at[n], e_r.at[n], across)

    loads = [
        pltpu.make_async_copy(head_hbm, heads, load_sem.at[0]),
        pltpu.make_async_copy(gate_hbm, gates, load_sem.at[1]),
        pltpu.make_async_copy(
            w_hbm.at[pl.ds(pl.multiple_of(core * 16, 16), 16)], w6.at[y, z, x, core], load_sem.at[2]
        ),
    ]
    for axis in range(2):
        for s in range(2):
            loads.append(
                pltpu.make_async_copy(
                    cot_hbm.at[:, pl.ds((axis * 2 + s) * SUB, SUB)],
                    cslot.at[axis, s, mine[axis]],
                    load_sem.at[3 + axis * 2 + s],
                )
            )
    loads += [
        pltpu.make_async_copy(cot_hbm, cot, load_sem.at[7]),
        pltpu.make_async_copy(mom_hbm, mom, load_sem.at[8]),
        pltpu.make_async_copy(idx_hbm, idx, load_sem.at[9]),
    ]
    for d in (1, 2, 3):
        wx(d).start()
    for load in loads[:3]:
        load.start()
    for axis in range(2):
        for way in range(2):
            first(axis, 0, way).start()
    for load in loads[3:]:
        load.start()

    row = lax.broadcasted_iota(jnp.int32, (SUB, SUB), 0)
    col = lax.broadcasted_iota(jnp.int32, (SUB, SUB), 1)
    source = ((row >> 5) & 3) * 128 + (row >> 7) * 32 + (row & 31)
    perm[0] = jnp.where(source == col, 1.0, 0.0).astype(BF16)
    perm[1] = jnp.where(row == col, 1.0, 0.0).astype(BF16)
    quarter, block = row >> 7, (row >> 4) & 7
    spread[...] = jnp.where((block == (col >> 6)) & (quarter == ((col >> 4) & 3)), 1.0, 0.0).astype(BF16)

    gain = gain_ref[...]
    loads[0].wait()
    loads[1].wait()

    def gated_rows(i, carry):
        rows = pl.ds(pl.multiple_of(i * 32, 32), 32)
        for k in range(WIDTH // HDIM):
            cols = slice(k * HDIM, (k + 1) * HDIM)
            h = heads[rows, cols].astype(F32)
            a = gates[rows, cols].astype(F32)
            n = h * lax.rsqrt(jnp.mean(h * h, axis=-1, keepdims=True) + EPS)
            low[rows, cols] = ((n * gain) * (a * jax.nn.sigmoid(a))).astype(BF16)
        return carry

    lax.fori_loop(0, 6, gated_rows, 0)

    loads[2].wait()
    for d in (1, 2, 3):
        wx(d).wait_recv()
    for d in (1, 2, 3):
        wy(d).start()

    @pl.when(lo == 1)
    def _():
        up(0).start()

    @pl.when(lo == 0)
    def _():
        down(0).start()

    to_sibling(0).start()

    lax.fori_loop(6, 12, gated_rows, 0)

    for axis in range(2):

        def turn(b, carry, axis=axis):
            part = low[:, pl.ds(pl.multiple_of(b * SUB, SUB), SUB)]
            out = lax.dot_general(
                perm[axis], part, (((1,), (1,)), ((), ())), preferred_element_type=F32
            ).astype(BF16)
            if axis == 0:
                for to in range(4):
                    gsend[0, to, pl.ds(pl.multiple_of(b * 128, 128), 128), :] = out[to * 128 : (to + 1) * 128]
            else:
                gsend[1, b] = out
            return carry

        lax.fori_loop(0, 4, turn, 0)
        for d in (2, 1, 3):
            gated_to(axis, d).start()
        own_gated(axis).start()

    for axis in range(2):
        for way in range(2):
            first(axis, 0, way).wait_recv()
        for way in range(2):
            second(axis, 0, way).start()
    for axis in range(2):
        for way in range(2):
            first(axis, 1, way).start()

    for d in (1, 2, 3):
        wy(d).wait_recv()

    @pl.when(lo == 1)
    def _():
        for p in (1, 2, 3):
            up(p).start()

    @pl.when(lo == 0)
    def _():
        for p in (1, 2, 3):
            down(p).start()

    for n in (1, 2, 3):
        to_sibling(n).start()

    def pass_on(p):
        up(p).wait_recv()

        @pl.when(lo == 0)
        def _():
            up(p).start()

        if p < 2:

            @pl.when(lo == 1)
            def _():
                up(p + 4).start()

        to_sibling(4 + p).start()
        down(p).wait_recv()

        @pl.when(lo == 1)
        def _():
            down(p).start()

        if p in (1, 2):

            @pl.when(lo == 0)
            def _():
                down(p + 3).start()

        to_sibling(10 + p).start()

    pass_on(0)

    def terms(n):
        axis, s = PIECES[n]
        right = cslot.at[axis, s]
        for d in (2, 1, 3, 0):
            owner = (mine[1 - axis] + d) % 4
            if axis == 0:
                left = gt[0, pl.ds(pl.multiple_of(owner * 128, 128), 128), :]
            else:
                left = jnp.concatenate(
                    [gt[1, pl.ds(pl.multiple_of(k * 128 + owner * 32, 32), 32), :] for k in range(4)], axis=0
                )
            part = jnp.dot(left, right[...].reshape(4 * TOK, SUB), preferred_element_type=F32)
            if d:
                p2s[n, d - 1] = part.astype(BF16)
                stage2(n, d).start()
            else:
                q[n] = part

    def pass_second(axis, s):
        for way in range(2):
            first(axis, s, way).wait_recv()
        for way in range(2):
            second(axis, s, way).start()

    def second_in(axis, s):
        for way in range(2):
            second(axis, s, way).wait_recv()

    def sum2(n):
        for d in (1, 2, 3):
            stage2(n, d).wait_recv()
        q[n] += (p2r[n, 0].astype(F32) + p2r[n, 1].astype(F32)) + p2r[n, 2].astype(F32)
        for d in (2, 1, 3):
            stage3(n, d).start()

    def gated_in(axis):
        own_gated(axis).wait()
        for d in (1, 2, 3):
            gated_to(axis, d).wait_recv()

    def moment_step(n):
        axis, s = PIECES[n]
        start = (axis * 2 + s) * SUB
        for d in (1, 2, 3):
            stage3(n, d).wait_recv()
        own = q[n, pl.ds(pl.multiple_of(z * ROWS, ROWS), ROWS), :]
        gradient = (own + p3r[n, 0]) + (p3r[n, 1] + p3r[n, 2])
        moment = DECAY * mom[:, start : start + SUB] + gradient * ((TOK * 64) ** -0.5)
        where = idx[:, start // 4 : start // 4 + 128]
        bits = jnp.left_shift(jnp.ones_like(where), where & 15)
        bits = jnp.concatenate(
            [jnp.where((where >> 4) == k, bits, 0).astype(F32).astype(BF16) for k in range(4)], axis=1
        )
        words = jnp.dot(bits, spread[...], preferred_element_type=F32).astype(jnp.int32)
        lane = lax.broadcasted_iota(jnp.int32, (ROWS, SUB), 1)
        chosen = (lax.shift_right_logical(words, lane & 15) & 1).astype(F32)

        def stacked(v):
            return jnp.concatenate([v[:, k * 128 : (k + 1) * 128] for k in range(4)], axis=0)

        coeffs = jnp.dot(stacked(moment), dct_ref[...], precision=HIGHEST, preferred_element_type=F32)
        decoded = jnp.dot(
            coeffs * stacked(chosen), idct_ref[...], precision=HIGHEST, preferred_element_type=F32
        )
        decoded = jnp.concatenate([decoded[k * ROWS : (k + 1) * ROWS] for k in range(4)], axis=1)
        dec[n] = decoded
        to_pair(n).start()
        newmom[n] = moment - decoded
        pltpu.make_async_copy(newmom.at[n], newmom_hbm.at[:, pl.ds(start, SUB)], out_sem.at[0, n]).start()

    def pair_step(n):
        to_pair(n).wait_recv()
        pair[n] = dec[n] + dec_r[n]
        to_across(n).start()

    def update_step(n):
        axis, s = PIECES[n]
        to_across(n).wait_recv()
        update[n] = (pair[n] + pair_r[n]) * 0.25
        start = (axis * 2 + s) * SUB
        pltpu.make_async_copy(update.at[n], update_hbm.at[:, pl.ds(start, SUB)], out_sem.at[1, n]).start()

    for load in loads[3:]:
        load.wait()
    for axis in range(2):
        gated_in(axis)
        second_in(axis, 0)
        terms(axis)
        pass_second(axis, 1)
        pass_on(1 + axis)
    sum2(0)
    sum2(1)
    pass_on(3)
    for axis in range(2):
        second_in(axis, 1)
        terms(2 + axis)
    pass_on(4)
    moment_step(0)
    moment_step(1)
    pass_on(5)
    sum2(2)
    sum2(3)
    pair_step(0)
    pair_step(1)

    for n in range(16):
        to_sibling(n).wait_recv()

    def grads_out(k, which):
        cols = pl.ds(pl.multiple_of(k * 256, 256), 256)
        src, dst = ((hgrad, hgrad_hbm), (ggrad, ggrad_hbm))[which]
        return pltpu.make_async_copy(src.at[k], dst.at[:, cols], out_sem.at[2 + which, k])

    def back(k, carry):
        weight = w6[k // 2, pl.ds((k % 2) * 2, 2)].reshape(256, WIDTH)
        upb[...] = lax.dot_general(
            cot[...], weight, (((1,), (1,)), ((), ())), preferred_element_type=F32
        )

        def back_rows(i, c):
            rows = pl.ds(pl.multiple_of(i * 32, 32), 32)
            for part in range(2):
                cols = pl.ds(pl.multiple_of(k * 256 + part * 128, 128), 128)
                here = slice(part * 128, (part + 1) * 128)
                h = heads[rows, cols].astype(F32)
                a = gates[rows, cols].astype(F32)
                u = upb[rows, here]
                r = lax.rsqrt(jnp.mean(h * h, axis=-1, keepdims=True) + EPS)
                n = h * r
                sig = jax.nn.sigmoid(a)
                ggrad[k, rows, here] = ((u * (n * gain)) * (sig * (1.0 + a * (1.0 - sig)))).astype(BF16)
                ds = (u * (a * sig)) * gain
                hgrad[k, rows, here] = (r * (ds - n * jnp.mean(ds * n, axis=-1, keepdims=True))).astype(BF16)
            return c

        lax.fori_loop(0, TOK // 32, back_rows, 0)
        grads_out(k, 0).start()
        grads_out(k, 1).start()
        return carry

    lax.fori_loop(0, 8, back, 0)

    for n in (2, 3):
        moment_step(n)
    update_step(0)
    update_step(1)
    for n in (2, 3):
        pair_step(n)
    for n in (2, 3):
        update_step(n)

    for d in (1, 2, 3):
        wx(d).wait_send()
        wy(d).wait_send()
        for axis in range(2):
            gated_to(axis, d).wait_send()
        for n in range(4):
            stage2(n, d).wait_send()
            stage3(n, d).wait_send()
    for p in range(6):
        up(p).wait_send()
        down(p).wait_send()
    for n in range(16):
        to_sibling(n).wait_send()
    for axis in range(2):
        for s in range(2):
            for way in range(2):
                first(axis, s, way).wait_send()
                second(axis, s, way).wait_send()
    for n in range(4):
        axis, s = PIECES[n]
        start = (axis * 2 + s) * SUB
        to_pair(n).wait_send()
        to_across(n).wait_send()
        pltpu.make_async_copy(newmom.at[n], newmom_hbm.at[:, pl.ds(start, SUB)], out_sem.at[0, n]).wait()
        pltpu.make_async_copy(update.at[n], update_hbm.at[:, pl.ds(start, SUB)], out_sem.at[1, n]).wait()
    for k in range(8):
        grads_out(k, 0).wait()
        grads_out(k, 1).wait()


def cosine_pair():
    freq = np.arange(SPAN)[:, None]
    place = np.arange(SPAN)[None, :]
    table = np.cos(np.pi * (place + 0.5) * freq / SPAN) * np.where(
        freq == 0, np.sqrt(1.0 / SPAN), np.sqrt(2.0 / SPAN)
    )
    inverse = np.kron(np.eye(2), table)
    return np.ascontiguousarray(inverse.T).astype(np.float32), inverse.astype(np.float32)


def local(head_out, gate_in, cotangent, momentum, chosen_index, out_weight, norm_gain):
    forward, inverse = cosine_pair()
    anywhere = pl.BlockSpec(memory_space=pl.ANY)
    vmem = pl.BlockSpec(memory_space=pltpu.VMEM)
    dma = pltpu.SemaphoreType.DMA
    scratch = [
        pltpu.VMEM((TOK, WIDTH), BF16),
        pltpu.VMEM((TOK, WIDTH), BF16),
        pltpu.VMEM((TOK, WIDTH), BF16),
        pltpu.VMEM((ROWS, WIDTH), F32),
        pltpu.VMEM((ROWS, WIDTH // 4), jnp.int32),
        pltpu.VMEM((4, 4, 4, 2, 16, WIDTH), BF16),
        pltpu.VMEM((TOK, WIDTH), BF16),
        pltpu.VMEM((2, 4, SUB, TOK), BF16),
        pltpu.VMEM((2, SUB, 4 * TOK), BF16),
        pltpu.VMEM((2, 2, 4, TOK, SUB), BF16),
        pltpu.VMEM((4, 3, 128, SUB), BF16),
        pltpu.VMEM((4, 3, 128, SUB), BF16),
        pltpu.VMEM((4, 128, SUB), F32),
        pltpu.VMEM((4, 3, ROWS, SUB), F32),
        pltpu.VMEM((4, ROWS, SUB), F32),
        pltpu.VMEM((4, ROWS, SUB), F32),
        pltpu.VMEM((4, ROWS, SUB), F32),
        pltpu.VMEM((4, ROWS, SUB), F32),
        pltpu.VMEM((4, ROWS, SUB), F32),
        pltpu.VMEM((4, ROWS, SUB), F32),
        pltpu.VMEM((2, SUB, SUB), BF16),
        pltpu.VMEM((SUB, SUB), BF16),
        pltpu.VMEM((TOK, 256), F32),
        pltpu.VMEM((8, TOK, 256), BF16),
        pltpu.VMEM((8, TOK, 256), BF16),
        dma((10,)), dma((2,)), dma((4, 8)),
        dma((3,)), dma((3,)), dma((3,)), dma((3,)),
        dma((6,)), dma((6,)), dma((6,)), dma((6,)),
        dma((16,)), dma((16,)),
        dma((2, 2, 2)), dma((2, 2, 2)), dma((2, 2, 2)), dma((2, 2, 2)),
        dma((2, 3)), dma((2, 3)),
        dma((4, 3)), dma((4, 3)), dma((4, 3)), dma((4, 3)),
        dma((4,)), dma((4,)), dma((4,)), dma((4,)),
    ]
    head_grad, gate_grad, new_momentum, update = pl.pallas_call(
        kernel,
        name="demo_step",
        out_shape=(
            jax.ShapeDtypeStruct((TOK, WIDTH), BF16),
            jax.ShapeDtypeStruct((TOK, WIDTH), BF16),
            jax.ShapeDtypeStruct((ROWS, WIDTH), F32),
            jax.ShapeDtypeStruct((ROWS, WIDTH), F32),
        ),
        in_specs=[anywhere] * 6 + [vmem] * 3,
        out_specs=(anywhere,) * 4,
        scratch_shapes=scratch,
        compiler_params=pltpu.CompilerParams(
            collective_id=0, has_side_effects=True, vmem_limit_bytes=56 * 2**20
        ),
        cost_estimate=pl.CostEstimate(flops=14 * 10**9, bytes_accessed=9 * 10**6, transcendentals=10**6),
    )(
        head_out[0], gate_in[0], cotangent[0], momentum[0], chosen_index[0], out_weight,
        norm_gain.reshape(1, HDIM), jnp.asarray(forward), jnp.asarray(inverse),
    )
    return head_grad[None], gate_grad[None], new_momentum[None], update


def solution(mesh):
    rows = P("group", "fsdp", None)
    return jax.shard_map(
        local,
        mesh=mesh,
        in_specs=(rows, rows, rows, rows, rows, P("fsdp", None), P()),
        out_specs=(rows, rows, rows, P("fsdp", None)),
        check_vma=False,
    )
```

time: 657 us -> 164 us (0.25)
  the two profiles are of different devices: /device:TPU:1 before, /device:TPU:242 now
where the time goes in v1:
time: 164 us
  Pallas kernels  158 us (96%)
  local copies, waits for them, and re-layouts  5.4 us (3%)
    pallas_call x1, Pallas kernels, local(): pl.pallas_call(kernel, name='demo_step', out_shape=(jax.ShapeDtypeStruct(...  158 us
    unnamed x10, local copies, waits for them, and re-layouts  5.4 us

profile of v1, /device:TPU:242, one launch (start us, length us, event | category | flops | bytes accessed | tf_op | source)
XLA Modules:
  0.0 164.1 jit_solution(1622606693987003444)
XLA Ops:
  0.6 158.0 %demo_step.1 = (bf16[384,2048]{1,0:T(8,128)(2,1)}, bf16[384,2048]{1,0:T(8,128)(2,1)}, f32[32,2048]{1,0:T(8,128)}, f32[32,2048]{1,0:T(8,128)}) custom-call(bf16[384,2048]{1,0:T(8,128)(2,1)} %bitcast.12, bf16[384,2048]{1,0:T(8,128)(2,1)} %bitcast.13, bf16[384,2048]{1,0:T(8,128)(2,1)} %bitcast.14, f32[32,2048]{1,0:T(8,128)} %bitcast.15, s32[32,512]{1,0:T(8,128)} %bitcast.16, ...), custom_call_target="tpu_custom_call" | custom-call | flops 14000000000 | bytes 9000000 | tf_op jit(solution)/shard_map/demo_step/pallas_call | solution.py:512
  158.7 0.0 copy-start
  158.7 2.8 %copy.17 = bf16[1,384,2048]{2,1,0:T(8,128)(2,1)} copy(bf16[1,384,2048]{2,1,0:T(8,128)(2,1)} %bitcast.10) | data formatting | bytes 3145728
  161.5 0.0 copy-done
  161.5 0.0 copy-start.2
  161.5 0.0 copy-start.1
  161.5 1.1 copy.18
  162.7 0.0 copy-done.2
  162.7 0.7 copy.19
  163.4 0.0 copy-done.1
  163.4 0.7 copy.20
Async XLA Ops:
  158.7 2.9 %copy-start = (bf16[384,2048]{1,0:T(8,128)(2,1)S(1)}, bf16[384,2048]{1,0:T(8,128)(2,1)}, u32[]{:S(2)}) copy-start(bf16[384,2048]{1,0:T(8,128)(2,1)} %get-tuple-element.9) | copy-start | bytes 4718596
  161.5 1.1 copy-start.2
  161.5 1.9 %copy-start.1 = (f32[32,2048]{1,0:T(8,128)S(1)}, f32[32,2048]{1,0:T(8,128)}, u32[]{:S(2)}) copy-start(f32[32,2048]{1,0:T(8,128)} %get-tuple-element.19) | copy-start | bytes 786436

commit v2 on v1

--- a/solution.py
+++ b/solution.py
@@ -24,7 +24,9 @@
 DECAY = 0.999
 
 PIECES = ((0, 0), (1, 0), (0, 1), (1, 1))
-DOWN_ORDER = (0, 2, 3, 1)
+
+UP_ORDER = (0, 1, 3, 2, 0, 1)
+DOWN_ORDER = (0, 3, 1, 2, 3, 2)
 
 
 def remote(src, dst, send, recv, device):
@@ -36,8 +38,8 @@
 def kernel(
     head_hbm, gate_hbm, cot_hbm, mom_hbm, idx_hbm, w_hbm, gain_ref, dct_ref, idct_ref,
     hgrad_hbm, ggrad_hbm, newmom_hbm, update_hbm,
-    heads, gates, cot, mom, idx, w6, low, gsend, gt, cslot, p2s, p2r, q, p3r, dec, dec_r, pair, pair_r,
-    newmom, update, perm, spread, upb, hgrad, ggrad,
+    heads, gates, cot, mom, idx, w6, low, gsend, gt, cslot, p2s, p2r, q, p3s, p3r, dec, dec_r, pair, pair_r,
+    newmom, update, perm, spread, hgrad, ggrad,
     load_sem, own_sem, out_sem,
     wx_s, wx_r, wy_s, wy_r, up_s, up_r, dn_s, dn_r, sib_s, sib_r,
     c1_s, c1_r, c2_s, c2_r, gt_s, gt_r, s2_s, s2_r, s3_s, s3_r, d_s, d_r, e_s, e_r,
@@ -78,28 +80,25 @@
         return remote(part, part, wy_s.at[d - 1], wy_r.at[d - 1], at_y(d))
 
     def up(p):
-        part = w6.at[(y + p % 4) % 4, (z + 8 - p // 4 - 1 + lo) % 4, :, core]
+        part = w6.at[(y + UP_ORDER[p]) % 4, (z + 8 - p // 4 - 1 + lo) % 4, :, core]
         return remote(part, part, up_s.at[p], up_r.at[p], above)
 
-    def down_piece(p):
-        return DOWN_ORDER[p] if p < 4 else p - 2
-
     def down(p):
-        part = w6.at[(y + down_piece(p)) % 4, (z + p // 4 + lo) % 4, :, core]
+        part = w6.at[(y + DOWN_ORDER[p]) % 4, (z + p // 4 + lo) % 4, :, core]
         return remote(part, part, dn_s.at[p], dn_r.at[p], below)
 
     def to_sibling(n):
         if n < 4:
             part = w6.at[(y + n) % 4, z, :, core]
         elif n < 10:
-            part = w6.at[(y + (n - 4) % 4) % 4, (z + 3 - (n - 4) // 4) % 4, :, core]
+            part = w6.at[(y + UP_ORDER[n - 4]) % 4, (z + 3 - (n - 4) // 4) % 4, :, core]
         else:
-            part = w6.at[(y + down_piece(n - 10)) % 4, (z + 1 + (n - 10) // 4) % 4, :, core]
+            part = w6.at[(y + DOWN_ORDER[n - 10]) % 4, (z + 1 + (n - 10) // 4) % 4, :, core]
         return remote(part, part, sib_s.at[n], sib_r.at[n], sibling)
 
     def first(axis, s, way):
-        src = cot_hbm.at[:, pl.ds((axis * 2 + s) * SUB, SUB)]
         dst = cslot.at[axis, s, mine[axis]]
+        src = dst if axis + s else cot_hbm.at[:, :SUB]
         return remote(src, dst, c1_s.at[axis, s, way], c1_r.at[axis, s, way], along[axis](1 + 2 * way))
 
     def second(axis, s, way):
@@ -122,8 +121,7 @@
         )
 
     def stage3(n, d):
-        src = q.at[n, pl.ds(pl.multiple_of(((z + d) % 4) * ROWS, ROWS), ROWS)]
-        return remote(src, p3r.at[n, d - 1], s3_s.at[n, d - 1], s3_r.at[n, d - 1], at_z(d))
+        return remote(p3s.at[n, d - 1], p3r.at[n, d - 1], s3_s.at[n, d - 1], s3_r.at[n, d - 1], at_z(d))
 
     def to_pair(n):
         return remote(dec.at[n], dec_r.at[n], d_s.at[n], d_r.at[n], sibling)
@@ -156,9 +154,8 @@
         wx(d).start()
     for load in loads[:3]:
         load.start()
-    for axis in range(2):
-        for way in range(2):
-            first(axis, 0, way).start()
+    for way in range(2):
+        first(0, 0, way).start()
     for load in loads[3:]:
         load.start()
 
@@ -184,13 +181,16 @@
             low[rows, cols] = ((n * gain) * (a * jax.nn.sigmoid(a))).astype(BF16)
         return carry
 
-    lax.fori_loop(0, 6, gated_rows, 0)
-
-    loads[2].wait()
+    lax.fori_loop(0, 3, gated_rows, 0)
+
+    for load in loads[2:]:
+        load.wait()
     for d in (1, 2, 3):
         wx(d).wait_recv()
-    for d in (1, 2, 3):
+    for d in (1, 3, 2):
         wy(d).start()
+    for way in range(2):
+        first(1, 0, way).start()
 
     @pl.when(lo == 1)
     def _():
@@ -202,7 +202,7 @@
 
     to_sibling(0).start()
 
-    lax.fori_loop(6, 12, gated_rows, 0)
+    lax.fori_loop(3, 12, gated_rows, 0)
 
     for axis in range(2):
 
@@ -223,60 +223,33 @@
             gated_to(axis, d).start()
         own_gated(axis).start()
 
-    for axis in range(2):
-        for way in range(2):
-            first(axis, 0, way).wait_recv()
-        for way in range(2):
-            second(axis, 0, way).start()
-    for axis in range(2):
-        for way in range(2):
-            first(axis, 1, way).start()
-
-    for d in (1, 2, 3):
-        wy(d).wait_recv()
-
-    @pl.when(lo == 1)
-    def _():
-        for p in (1, 2, 3):
-            up(p).start()
-
-    @pl.when(lo == 0)
-    def _():
-        for p in (1, 2, 3):
-            down(p).start()
-
-    for n in (1, 2, 3):
-        to_sibling(n).start()
-
-    def pass_on(p):
-        up(p).wait_recv()
-
+    def relay(p):
         @pl.when(lo == 0)
         def _():
+            up(p).wait_recv()
             up(p).start()
-
-        if p < 2:
-
-            @pl.when(lo == 1)
-            def _():
-                up(p + 4).start()
-
-        to_sibling(4 + p).start()
-        down(p).wait_recv()
+            to_sibling(4 + p).start()
 
         @pl.when(lo == 1)
         def _():
+            down(p).wait_recv()
             down(p).start()
-
-        if p in (1, 2):
-
-            @pl.when(lo == 0)
-            def _():
-                down(p + 3).start()
-
-        to_sibling(10 + p).start()
-
-    pass_on(0)
+            to_sibling(10 + p).start()
+
+    def follow(p):
+        @pl.when(lo == 0)
+        def _():
+            down(p).wait_recv()
+            if p in (1, 3):
+                down(p // 2 + 4).start()
+            to_sibling(10 + p).start()
+
+        @pl.when(lo == 1)
+        def _():
+            up(p).wait_recv()
+            if p < 2:
+                up(p + 4).start()
+            to_sibling(4 + p).start()
 
     def terms(n):
         axis, s = PIECES[n]
@@ -299,8 +272,18 @@
     def pass_second(axis, s):
         for way in range(2):
             first(axis, s, way).wait_recv()
-        for way in range(2):
             second(axis, s, way).start()
+
+    def own_piece(j):
+        @pl.when(lo == 1)
+        def _():
+            up(UP_ORDER.index(j)).start()
+
+        @pl.when(lo == 0)
+        def _():
+            down(DOWN_ORDER.index(j)).start()
+
+        to_sibling(j).start()
 
     def second_in(axis, s):
         for way in range(2):
@@ -311,6 +294,8 @@
             stage2(n, d).wait_recv()
         q[n] += (p2r[n, 0].astype(F32) + p2r[n, 1].astype(F32)) + p2r[n, 2].astype(F32)
         for d in (2, 1, 3):
+            rows = pl.ds(pl.multiple_of(((z + d) % 4) * ROWS, ROWS), ROWS)
+            p3s[n, d - 1] = q[n, rows, :].astype(BF16)
             stage3(n, d).start()
 
     def gated_in(axis):
@@ -324,7 +309,7 @@
         for d in (1, 2, 3):
             stage3(n, d).wait_recv()
         own = q[n, pl.ds(pl.multiple_of(z * ROWS, ROWS), ROWS), :]
-        gradient = (own + p3r[n, 0]) + (p3r[n, 1] + p3r[n, 2])
+        gradient = (own + p3r[n, 0].astype(F32)) + (p3r[n, 1].astype(F32) + p3r[n, 2].astype(F32))
         moment = DECAY * mom[:, start : start + SUB] + gradient * ((TOK * 64) ** -0.5)
         where = idx[:, start // 4 : start // 4 + 128]
         bits = jnp.left_shift(jnp.ones_like(where), where & 15)
@@ -360,74 +345,101 @@
         start = (axis * 2 + s) * SUB
         pltpu.make_async_copy(update.at[n], update_hbm.at[:, pl.ds(start, SUB)], out_sem.at[1, n]).start()
 
-    for load in loads[3:]:
-        load.wait()
-    for axis in range(2):
-        gated_in(axis)
-        second_in(axis, 0)
-        terms(axis)
-        pass_second(axis, 1)
-        pass_on(1 + axis)
-    sum2(0)
-    sum2(1)
-    pass_on(3)
-    for axis in range(2):
-        second_in(axis, 1)
-        terms(2 + axis)
-    pass_on(4)
-    moment_step(0)
-    moment_step(1)
-    pass_on(5)
-    sum2(2)
-    sum2(3)
-    pair_step(0)
-    pair_step(1)
-
-    for n in range(16):
-        to_sibling(n).wait_recv()
-
-    def grads_out(k, which):
-        cols = pl.ds(pl.multiple_of(k * 256, 256), 256)
+    def grads_out(which, head):
+        cols = pl.ds(pl.multiple_of(head * HDIM, HDIM), HDIM)
         src, dst = ((hgrad, hgrad_hbm), (ggrad, ggrad_hbm))[which]
-        return pltpu.make_async_copy(src.at[k], dst.at[:, cols], out_sem.at[2 + which, k])
-
-    def back(k, carry):
-        weight = w6[k // 2, pl.ds((k % 2) * 2, 2)].reshape(256, WIDTH)
-        upb[...] = lax.dot_general(
-            cot[...], weight, (((1,), (1,)), ((), ())), preferred_element_type=F32
-        )
-
-        def back_rows(i, c):
-            rows = pl.ds(pl.multiple_of(i * 32, 32), 32)
+        return pltpu.make_async_copy(src.at[:, cols], dst.at[:, cols], out_sem.at[2 + which, head])
+
+    def back(block, pieces, arrivals):
+        for n in arrivals:
+            to_sibling(n).wait_recv()
+        ys = [(y + j) % 4 for j in pieces]
+
+        def back_rows(i, carry):
+            rows = pl.ds(pl.multiple_of(i * 128, 128), 128)
+            weight = jnp.concatenate([w6[v, block].reshape(HDIM, WIDTH) for v in ys], axis=0)
+            both = lax.dot_general(
+                cot[rows, :], weight, (((1,), (1,)), ((), ())), preferred_element_type=F32
+            )
             for part in range(2):
-                cols = pl.ds(pl.multiple_of(k * 256 + part * 128, 128), 128)
-                here = slice(part * 128, (part + 1) * 128)
+                cols = pl.ds(pl.multiple_of((ys[part] * 4 + block) * HDIM, HDIM), HDIM)
+                u = both[:, part * HDIM : (part + 1) * HDIM]
                 h = heads[rows, cols].astype(F32)
                 a = gates[rows, cols].astype(F32)
-                u = upb[rows, here]
                 r = lax.rsqrt(jnp.mean(h * h, axis=-1, keepdims=True) + EPS)
                 n = h * r
                 sig = jax.nn.sigmoid(a)
-                ggrad[k, rows, here] = ((u * (n * gain)) * (sig * (1.0 + a * (1.0 - sig)))).astype(BF16)
+                ggrad[rows, cols] = ((u * (n * gain)) * (sig * (1.0 + a * (1.0 - sig)))).astype(BF16)
                 ds = (u * (a * sig)) * gain
-                hgrad[k, rows, here] = (r * (ds - n * jnp.mean(ds * n, axis=-1, keepdims=True))).astype(BF16)
-            return c
-
-        lax.fori_loop(0, TOK // 32, back_rows, 0)
-        grads_out(k, 0).start()
-        grads_out(k, 1).start()
-        return carry
-
-    lax.fori_loop(0, 8, back, 0)
-
-    for n in (2, 3):
-        moment_step(n)
+                hgrad[rows, cols] = (r * (ds - n * jnp.mean(ds * n, axis=-1, keepdims=True))).astype(BF16)
+            return carry
+
+        lax.fori_loop(0, TOK // 128, back_rows, 0)
+        for v in ys:
+            grads_out(0, v * 4 + block).start()
+            grads_out(1, v * 4 + block).start()
+
+    prev, prev2, after = (z + 3) % 4, (z + 2) % 4, (z + 1) % 4
+
+    relay(0)
+    for j in (1, 3):
+        wy(4 - j).wait_recv()
+        own_piece(j)
+    pass_second(0, 0)
+    for way in range(2):
+        first(0, 1, way).start()
+    wy(2).wait_recv()
+    own_piece(2)
+    follow(0)
+    back(z, (0, 1), (0, 1))
+    relay(1)
+    pass_second(1, 0)
+    for way in range(2):
+        first(1, 1, way).start()
+    back(z, (2, 3), (2, 3))
+    relay(2)
+    follow(1)
+    gated_in(0)
+    second_in(0, 0)
+    terms(0)
+    relay(3)
+    follow(2)
+    back(prev, (0, 1), (4, 5))
+    relay(4)
+    follow(3)
+    pass_second(0, 1)
+    gated_in(1)
+    second_in(1, 0)
+    terms(1)
+    relay(5)
+    follow(4)
+    back(after, (2, 3), (11, 13))
+    pass_second(1, 1)
+    second_in(0, 1)
+    terms(2)
+    follow(5)
+    sum2(1)
+    back(prev, (2, 3), (6, 7))
+    sum2(0)
+    back(after, (0, 1), (10, 12))
+    moment_step(1)
+    second_in(1, 1)
+    terms(3)
+    moment_step(0)
+    pair_step(1)
+    back(prev2, (0, 1), (8, 9))
+    pair_step(0)
+    sum2(2)
+    sum2(3)
     update_step(0)
     update_step(1)
-    for n in (2, 3):
-        pair_step(n)
-    for n in (2, 3):
-        update_step(n)
+    back(prev2, (2, 3), (14, 15))
+    moment_step(2)
+    moment_step(3)
+    pair_step(2)
+    pair_step(3)
+    update_step(2)
+    update_step(3)
 
     for d in (1, 2, 3):
         wx(d).wait_send()
@@ -454,9 +466,9 @@
         to_across(n).wait_send()
         pltpu.make_async_copy(newmom.at[n], newmom_hbm.at[:, pl.ds(start, SUB)], out_sem.at[0, n]).wait()
         pltpu.make_async_copy(update.at[n], update_hbm.at[:, pl.ds(start, SUB)], out_sem.at[1, n]).wait()
-    for k in range(8):
-        grads_out(k, 0).wait()
-        grads_out(k, 1).wait()
+    for head in range(16):
+        grads_out(0, head).wait()
+        grads_out(1, head).wait()
 
 
 def cosine_pair():
@@ -488,7 +500,8 @@
         pltpu.VMEM((4, 3, 128, SUB), BF16),
         pltpu.VMEM((4, 3, 128, SUB), BF16),
         pltpu.VMEM((4, 128, SUB), F32),
-        pltpu.VMEM((4, 3, ROWS, SUB), F32),
+        pltpu.VMEM((4, 3, ROWS, SUB), BF16),
+        pltpu.VMEM((4, 3, ROWS, SUB), BF16),
         pltpu.VMEM((4, ROWS, SUB), F32),
         pltpu.VMEM((4, ROWS, SUB), F32),
         pltpu.VMEM((4, ROWS, SUB), F32),
@@ -497,10 +510,9 @@
         pltpu.VMEM((4, ROWS, SUB), F32),
         pltpu.VMEM((2, SUB, SUB), BF16),
         pltpu.VMEM((SUB, SUB), BF16),
-        pltpu.VMEM((TOK, 256), F32),
-        pltpu.VMEM((8, TOK, 256), BF16),
-        pltpu.VMEM((8, TOK, 256), BF16),
-        dma((10,)), dma((2,)), dma((4, 8)),
+        pltpu.VMEM((TOK, WIDTH), BF16),
+        pltpu.VMEM((TOK, WIDTH), BF16),
+        dma((10,)), dma((2,)), dma((4, 16)),
         dma((3,)), dma((3,)), dma((3,)), dma((3,)),
         dma((6,)), dma((6,)), dma((6,)), dma((6,)),
         dma((16,)), dma((16,)),

time: 164 us -> 109 us (0.66)
  the two profiles are of different devices: /device:TPU:242 before, /device:TPU:1 now
where the time goes in v2:
time: 109 us; the launch traced here: 108 us
  Pallas kernels  102 us (94%)
  local copies, waits for them, and re-layouts  5.4 us (5%)
    pallas_call x1, Pallas kernels, local(): pl.pallas_call(kernel, name='demo_step', out_shape=(jax.ShapeDtypeStruct(...  102 us
    unnamed x10, local copies, waits for them, and re-layouts  5.4 us

profile of v2, /device:TPU:1, one launch (start us, length us, event | category | flops | bytes accessed | tf_op | source)
XLA Modules:
  0.0 108.5 jit_solution(8378950872516257669)
XLA Ops:
  0.6 102.4 %demo_step.1 = (bf16[384,2048]{1,0:T(8,128)(2,1)}, bf16[384,2048]{1,0:T(8,128)(2,1)}, f32[32,2048]{1,0:T(8,128)}, f32[32,2048]{1,0:T(8,128)}) custom-call(bf16[384,2048]{1,0:T(8,128)(2,1)} %bitcast.12, bf16[384,2048]{1,0:T(8,128)(2,1)} %bitcast.13, bf16[384,2048]{1,0:T(8,128)(2,1)} %bitcast.14, f32[32,2048]{1,0:T(8,128)} %bitcast.15, s32[32,512]{1,0:T(8,128)} %bitcast.16, ...), custom_call_target="tpu_custom_call" | custom-call | flops 14000000000 | bytes 9000000 | tf_op jit(solution)/shard_map/demo_step/pallas_call | solution.py:524
  103.1 0.0 copy-start
  103.1 2.8 %copy.17 = bf16[1,384,2048]{2,1,0:T(8,128)(2,1)} copy(bf16[1,384,2048]{2,1,0:T(8,128)(2,1)} %bitcast.10) | data formatting | bytes 3145728
  105.9 0.0 copy-done
  105.9 0.0 copy-start.2
  105.9 0.0 copy-start.1
  105.9 1.1 %copy.18 = bf16[1,384,2048]{2,1,0:T(8,128)(2,1)} copy(bf16[1,384,2048]{2,1,0:T(8,128)(2,1)S(1)} %bitcast.9) | data formatting | bytes 3145728
  107.1 0.0 copy-done.2
  107.1 0.7 copy.19
  107.8 0.0 copy-done.1
  107.8 0.7 copy.20
Async XLA Ops:
  103.1 2.9 %copy-start = (bf16[384,2048]{1,0:T(8,128)(2,1)S(1)}, bf16[384,2048]{1,0:T(8,128)(2,1)}, u32[]{:S(2)}) copy-start(bf16[384,2048]{1,0:T(8,128)(2,1)} %get-tuple-element.9) | copy-start | bytes 4718596
  105.9 1.1 %copy-start.2 = (f32[32,2048]{1,0:T(8,128)S(1)}, f32[32,2048]{1,0:T(8,128)}, u32[]{:S(2)}) copy-start(f32[32,2048]{1,0:T(8,128)} %get-tuple-element.10) | copy-start | bytes 786436
  105.9 1.9 %copy-start.1 = (f32[32,2048]{1,0:T(8,128)S(1)}, f32[32,2048]{1,0:T(8,128)}, u32[]{:S(2)}) copy-start(f32[32,2048]{1,0:T(8,128)} %get-tuple-element.19) | copy-start | bytes 786436

commit v3 on v2

--- a/solution.py
+++ b/solution.py
@@ -37,10 +37,10 @@
 
 def kernel(
     head_hbm, gate_hbm, cot_hbm, mom_hbm, idx_hbm, w_hbm, gain_ref, dct_ref, idct_ref,
-    hgrad_hbm, ggrad_hbm, newmom_hbm, update_hbm,
-    heads, gates, cot, mom, idx, w6, low, gsend, gt, cslot, p2s, p2r, q, p3s, p3r, dec, dec_r, pair, pair_r,
-    newmom, update, perm, spread, hgrad, ggrad,
-    load_sem, own_sem, out_sem,
+    hgrad, ggrad, newmom, update,
+    heads, gates, cot, mom, idx, w6, gsend, gt, cslot, p2s, p2r, q, p3s, p3r, dec, dec_r, pair, pair_r,
+    spread,
+    load_sem, own_sem,
     wx_s, wx_r, wy_s, wy_r, up_s, up_r, dn_s, dn_r, sib_s, sib_r,
     c1_s, c1_r, c2_s, c2_r, gt_s, gt_r, s2_s, s2_r, s3_s, s3_r, d_s, d_r, e_s, e_r,
 ):
@@ -96,10 +96,12 @@
             part = w6.at[(y + DOWN_ORDER[n - 10]) % 4, (z + 1 + (n - 10) // 4) % 4, :, core]
         return remote(part, part, sib_s.at[n], sib_r.at[n], sibling)
 
-    def first(axis, s, way):
-        dst = cslot.at[axis, s, mine[axis]]
-        src = dst if axis + s else cot_hbm.at[:, :SUB]
-        return remote(src, dst, c1_s.at[axis, s, way], c1_r.at[axis, s, way], along[axis](1 + 2 * way))
+    def first(axis, s, way, half):
+        rows = pl.ds(half * (TOK // 2), TOK // 2)
+        dst = cslot.at[axis, s, mine[axis], rows]
+        src = dst if s else cot_hbm.at[rows, pl.ds(axis * 2 * SUB, SUB)]
+        sems = axis, s, way, half
+        return remote(src, dst, c1_s.at[sems], c1_r.at[sems], along[axis](1 + 2 * way))
 
     def second(axis, s, way):
         part = cslot.at[axis, s, (mine[axis] + 3 + 2 * way) % 4, pl.ds(way * (TOK // 2), TOK // 2)]
@@ -155,15 +157,15 @@
     for load in loads[:3]:
         load.start()
     for way in range(2):
-        first(0, 0, way).start()
+        first(0, 0, way, way).start()
+        first(1, 0, way, way).start()
+    for way in range(2):
+        first(0, 0, way, 1 - way).start()
     for load in loads[3:]:
         load.start()
 
     row = lax.broadcasted_iota(jnp.int32, (SUB, SUB), 0)
     col = lax.broadcasted_iota(jnp.int32, (SUB, SUB), 1)
-    source = ((row >> 5) & 3) * 128 + (row >> 7) * 32 + (row & 31)
-    perm[0] = jnp.where(source == col, 1.0, 0.0).astype(BF16)
-    perm[1] = jnp.where(row == col, 1.0, 0.0).astype(BF16)
     quarter, block = row >> 7, (row >> 4) & 7
     spread[...] = jnp.where((block == (col >> 6)) & (quarter == ((col >> 4) & 3)), 1.0, 0.0).astype(BF16)
 
@@ -171,17 +173,21 @@
     loads[0].wait()
     loads[1].wait()
 
-    def gated_rows(i, carry):
-        rows = pl.ds(pl.multiple_of(i * 32, 32), 32)
-        for k in range(WIDTH // HDIM):
-            cols = slice(k * HDIM, (k + 1) * HDIM)
-            h = heads[rows, cols].astype(F32)
-            a = gates[rows, cols].astype(F32)
+    def gated_block(b, carry):
+        for k in range(4):
+            cols = pl.ds(pl.multiple_of(b * SUB + k * HDIM, HDIM), HDIM)
+            h = heads[:, cols].astype(F32)
+            a = gates[:, cols].astype(F32)
             n = h * lax.rsqrt(jnp.mean(h * h, axis=-1, keepdims=True) + EPS)
-            low[rows, cols] = ((n * gain) * (a * jax.nn.sigmoid(a))).astype(BF16)
+            low = ((n * gain) * (a * jax.nn.sigmoid(a))).astype(BF16)
+            turned = low.T
+            gsend[1, b, k * 128 : (k + 1) * 128, :] = turned
+            for to in range(4):
+                rows = pl.ds(pl.multiple_of(b * 128 + k * 32, 32), 32)
+                gsend[0, to, rows, :] = turned[to * 32 : (to + 1) * 32]
         return carry
 
-    lax.fori_loop(0, 3, gated_rows, 0)
+    lax.fori_loop(0, 1, gated_block, 0)
 
     for load in loads[2:]:
         load.wait()
@@ -190,7 +196,7 @@
     for d in (1, 3, 2):
         wy(d).start()
     for way in range(2):
-        first(1, 0, way).start()
+        first(1, 0, way, 1 - way).start()
 
     @pl.when(lo == 1)
     def _():
@@ -202,25 +208,11 @@
 
     to_sibling(0).start()
 
-    lax.fori_loop(3, 12, gated_rows, 0)
-
+    lax.fori_loop(1, 4, gated_block, 0)
+    for d in (2, 1, 3):
+        for axis in range(2):
+            gated_to(axis, d).start()
     for axis in range(2):
-
-        def turn(b, carry, axis=axis):
-            part = low[:, pl.ds(pl.multiple_of(b * SUB, SUB), SUB)]
-            out = lax.dot_general(
-                perm[axis], part, (((1,), (1,)), ((), ())), preferred_element_type=F32
-            ).astype(BF16)
-            if axis == 0:
-                for to in range(4):
-                    gsend[0, to, pl.ds(pl.multiple_of(b * 128, 128), 128), :] = out[to * 128 : (to + 1) * 128]
-            else:
-                gsend[1, b] = out
-            return carry
-
-        lax.fori_loop(0, 4, turn, 0)
-        for d in (2, 1, 3):
-            gated_to(axis, d).start()
         own_gated(axis).start()
 
     def relay(p):
@@ -253,25 +245,24 @@
 
     def terms(n):
         axis, s = PIECES[n]
-        right = cslot.at[axis, s]
-        for d in (2, 1, 3, 0):
-            owner = (mine[1 - axis] + d) % 4
-            if axis == 0:
-                left = gt[0, pl.ds(pl.multiple_of(owner * 128, 128), 128), :]
-            else:
-                left = jnp.concatenate(
-                    [gt[1, pl.ds(pl.multiple_of(k * 128 + owner * 32, 32), 32), :] for k in range(4)], axis=0
-                )
-            part = jnp.dot(left, right[...].reshape(4 * TOK, SUB), preferred_element_type=F32)
-            if d:
-                p2s[n, d - 1] = part.astype(BF16)
-                stage2(n, d).start()
-            else:
-                q[n] = part
+        owners = [(mine[1 - axis] + d) % 4 for d in (1, 2, 3, 0)]
+        if axis == 0:
+            starts = [owner * 128 for owner in owners]
+            left = [gt[0, pl.ds(pl.multiple_of(v, 128), 128), :] for v in starts]
+        else:
+            starts = [k * 128 + owner * 32 for owner in owners for k in range(4)]
+            left = [gt[1, pl.ds(pl.multiple_of(v, 32), 32), :] for v in starts]
+        part = jnp.dot(
+            jnp.concatenate(left, axis=0), cslot[axis, s].reshape(4 * TOK, SUB), preferred_element_type=F32
+        )
+        for d in (2, 1, 3):
+            p2s[n, d - 1] = part[(d - 1) * 128 : d * 128].astype(BF16)
+            stage2(n, d).start()
+        q[n] = part[384:]
 
     def pass_second(axis, s):
         for way in range(2):
-            first(axis, s, way).wait_recv()
+            first(axis, s, way, way).wait_recv()
             second(axis, s, way).start()
 
     def own_piece(j):
@@ -287,6 +278,7 @@
 
     def second_in(axis, s):
         for way in range(2):
+            first(axis, s, way, 1 - way).wait_recv()
             second(axis, s, way).wait_recv()
 
     def sum2(n):
@@ -330,8 +322,7 @@
         decoded = jnp.concatenate([decoded[k * ROWS : (k + 1) * ROWS] for k in range(4)], axis=1)
         dec[n] = decoded
         to_pair(n).start()
-        newmom[n] = moment - decoded
-        pltpu.make_async_copy(newmom.at[n], newmom_hbm.at[:, pl.ds(start, SUB)], out_sem.at[0, n]).start()
+        newmom[:, start : start + SUB] = moment - decoded
 
     def pair_step(n):
         to_pair(n).wait_recv()
@@ -341,43 +332,28 @@
     def update_step(n):
         axis, s = PIECES[n]
         to_across(n).wait_recv()
-        update[n] = (pair[n] + pair_r[n]) * 0.25
         start = (axis * 2 + s) * SUB
-        pltpu.make_async_copy(update.at[n], update_hbm.at[:, pl.ds(start, SUB)], out_sem.at[1, n]).start()
-
-    def grads_out(which, head):
-        cols = pl.ds(pl.multiple_of(head * HDIM, HDIM), HDIM)
-        src, dst = ((hgrad, hgrad_hbm), (ggrad, ggrad_hbm))[which]
-        return pltpu.make_async_copy(src.at[:, cols], dst.at[:, cols], out_sem.at[2 + which, head])
+        update[:, start : start + SUB] = (pair[n] + pair_r[n]) * 0.25
 
     def back(block, pieces, arrivals):
         for n in arrivals:
             to_sibling(n).wait_recv()
         ys = [(y + j) % 4 for j in pieces]
 
-        def back_rows(i, carry):
-            rows = pl.ds(pl.multiple_of(i * 128, 128), 128)
-            weight = jnp.concatenate([w6[v, block].reshape(HDIM, WIDTH) for v in ys], axis=0)
-            both = lax.dot_general(
-                cot[rows, :], weight, (((1,), (1,)), ((), ())), preferred_element_type=F32
-            )
-            for part in range(2):
-                cols = pl.ds(pl.multiple_of((ys[part] * 4 + block) * HDIM, HDIM), HDIM)
-                u = both[:, part * HDIM : (part + 1) * HDIM]
-                h = heads[rows, cols].astype(F32)
-                a = gates[rows, cols].astype(F32)
-                r = lax.rsqrt(jnp.mean(h * h, axis=-1, keepdims=True) + EPS)
-                n = h * r
-                sig = jax.nn.sigmoid(a)
-                ggrad[rows, cols] = ((u * (n * gain)) * (sig * (1.0 + a * (1.0 - sig)))).astype(BF16)
-                ds = (u * (a * sig)) * gain
-                hgrad[rows, cols] = (r * (ds - n * jnp.mean(ds * n, axis=-1, keepdims=True))).astype(BF16)
-            return carry
-
-        lax.fori_loop(0, TOK // 128, back_rows, 0)
-        for v in ys:
-            grads_out(0, v * 4 + block).start()
-            grads_out(1, v * 4 + block).start()
+        weight = jnp.concatenate([w6[v, block].reshape(HDIM, WIDTH) for v in ys], axis=0)
+        both = lax.dot_general(cot[...], weight, (((1,), (1,)), ((), ())), preferred_element_type=F32)
+        for part in range(2):
+            head = ys[part] * 4 + block
+            cols = pl.ds(pl.multiple_of(head * HDIM, HDIM), HDIM)
+            u = both[:, part * HDIM : (part + 1) * HDIM]
+            h = heads[:, cols].astype(F32)
+            a = gates[:, cols].astype(F32)
+            r = lax.rsqrt(jnp.mean(h * h, axis=-1, keepdims=True) + EPS)
+            n = h * r
+            sig = jax.nn.sigmoid(a)
+            ggrad[:, cols] = ((u * (n * gain)) * (sig * (1.0 + a * (1.0 - sig)))).astype(BF16)
+            ds = (u * (a * sig)) * gain
+            hgrad[:, cols] = (r * (ds - n * jnp.mean(ds * n, axis=-1, keepdims=True))).astype(BF16)
 
     prev, prev2, after = (z + 3) % 4, (z + 2) % 4, (z + 1) % 4
 
@@ -386,16 +362,18 @@
         wy(4 - j).wait_recv()
         own_piece(j)
     pass_second(0, 0)
-    for way in range(2):
-        first(0, 1, way).start()
+    for half in range(2):
+        for way in range(2):
+            first(0, 1, way, (way + half) % 2).start()
     wy(2).wait_recv()
     own_piece(2)
     follow(0)
     back(z, (0, 1), (0, 1))
     relay(1)
     pass_second(1, 0)
-    for way in range(2):
-        first(1, 1, way).start()
+    for half in range(2):
+        for way in range(2):
+            first(1, 1, way, (way + half) % 2).start()
     back(z, (2, 3), (2, 3))
     relay(2)
     follow(1)
@@ -457,18 +435,28 @@
     for axis in range(2):
         for s in range(2):
             for way in range(2):
-                first(axis, s, way).wait_send()
+                first(axis, s, way, 0).wait_send()
+                first(axis, s, way, 1).wait_send()
                 second(axis, s, way).wait_send()
     for n in range(4):
-        axis, s = PIECES[n]
-        start = (axis * 2 + s) * SUB
         to_pair(n).wait_send()
         to_across(n).wait_send()
-        pltpu.make_async_copy(newmom.at[n], newmom_hbm.at[:, pl.ds(start, SUB)], out_sem.at[0, n]).wait()
-        pltpu.make_async_copy(update.at[n], update_hbm.at[:, pl.ds(start, SUB)], out_sem.at[1, n]).wait()
-    for head in range(16):
-        grads_out(0, head).wait()
-        grads_out(1, head).wait()
+
+
+def place(*refs):
+    sources, targets, sem = refs[:4], refs[4:8], refs[8]
+    copies = []
+    for n in range(4):
+        rows = sources[n].shape[0] // 2
+        for half in range(2):
+            part = pl.ds(half * rows, rows)
+            copies.append(
+                pltpu.make_async_copy(sources[n].at[part], targets[n].at[part], sem.at[n * 2 + half])
+            )
+    for copy in copies:
+        copy.start()
+    for copy in copies:
+        copy.wait()
 
 
 def cosine_pair():
@@ -493,7 +481,6 @@
         pltpu.VMEM((ROWS, WIDTH), F32),
         pltpu.VMEM((ROWS, WIDTH // 4), jnp.int32),
         pltpu.VMEM((4, 4, 4, 2, 16, WIDTH), BF16),
-        pltpu.VMEM((TOK, WIDTH), BF16),
         pltpu.VMEM((2, 4, SUB, TOK), BF16),
         pltpu.VMEM((2, SUB, 4 * TOK), BF16),
         pltpu.VMEM((2, 2, 4, TOK, SUB), BF16),
@@ -506,41 +493,45 @@
         pltpu.VMEM((4, ROWS, SUB), F32),
         pltpu.VMEM((4, ROWS, SUB), F32),
         pltpu.VMEM((4, ROWS, SUB), F32),
-        pltpu.VMEM((4, ROWS, SUB), F32),
-        pltpu.VMEM((4, ROWS, SUB), F32),
-        pltpu.VMEM((2, SUB, SUB), BF16),
         pltpu.VMEM((SUB, SUB), BF16),
-        pltpu.VMEM((TOK, WIDTH), BF16),
-        pltpu.VMEM((TOK, WIDTH), BF16),
-        dma((10,)), dma((2,)), dma((4, 16)),
+        dma((10,)), dma((2,)),
         dma((3,)), dma((3,)), dma((3,)), dma((3,)),
         dma((6,)), dma((6,)), dma((6,)), dma((6,)),
         dma((16,)), dma((16,)),
-        dma((2, 2, 2)), dma((2, 2, 2)), dma((2, 2, 2)), dma((2, 2, 2)),
+        dma((2, 2, 2, 2)), dma((2, 2, 2, 2)), dma((2, 2, 2)), dma((2, 2, 2)),
         dma((2, 3)), dma((2, 3)),
         dma((4, 3)), dma((4, 3)), dma((4, 3)), dma((4, 3)),
         dma((4,)), dma((4,)), dma((4,)), dma((4,)),
     ]
-    head_grad, gate_grad, new_momentum, update = pl.pallas_call(
+    results = pl.pallas_call(
         kernel,
         name="demo_step",
         out_shape=(
-            jax.ShapeDtypeStruct((TOK, WIDTH), BF16),
-            jax.ShapeDtypeStruct((TOK, WIDTH), BF16),
-            jax.ShapeDtypeStruct((ROWS, WIDTH), F32),
-            jax.ShapeDtypeStruct((ROWS, WIDTH), F32),
+            pltpu.VMEM((TOK, WIDTH), BF16),
+            pltpu.VMEM((TOK, WIDTH), BF16),
+            pltpu.VMEM((ROWS, WIDTH), F32),
+            pltpu.VMEM((ROWS, WIDTH), F32),
         ),
         in_specs=[anywhere] * 6 + [vmem] * 3,
-        out_specs=(anywhere,) * 4,
+        out_specs=(vmem,) * 4,
         scratch_shapes=scratch,
         compiler_params=pltpu.CompilerParams(
-            collective_id=0, has_side_effects=True, vmem_limit_bytes=56 * 2**20
+            collective_id=0, has_side_effects=True, vmem_limit_bytes=60 * 2**20 + 2**18
         ),
         cost_estimate=pl.CostEstimate(flops=14 * 10**9, bytes_accessed=9 * 10**6, transcendentals=10**6),
     )(
         head_out[0], gate_in[0], cotangent[0], momentum[0], chosen_index[0], out_weight,
         norm_gain.reshape(1, HDIM), jnp.asarray(forward), jnp.asarray(inverse),
     )
+    head_grad, gate_grad, new_momentum, update = pl.pallas_call(
+        place,
+        name="place_results",
+        out_shape=tuple(jax.ShapeDtypeStruct(v.shape, v.dtype) for v in results),
+        in_specs=[vmem] * 4,
+        out_specs=(anywhere,) * 4,
+        scratch_shapes=[dma((8,))],
+        compiler_params=pltpu.CompilerParams(vmem_limit_bytes=2**20),
+    )(*(pltpu.with_memory_space_constraint(v, pltpu.VMEM) for v in results))
     return head_grad[None], gate_grad[None], new_momentum[None], update
 
 

time: 109 us -> 100 us (0.917)
  local copies, waits for them, and re-layouts: 5.4 us -> 0 us
  Pallas kernels: 102 us -> 99.3 us
    unnamed x10 -> x0, local copies, waits for them, and re-layouts: 5.4 us -> none
    pallas_call x1 -> x2, Pallas kernels: 102 us -> 99.3 us  [the longest x1 97.4 us: local(): pl.pallas_call(kernel, name='demo_step', out_shape=(pltpu.VMEM((TOK, WIDT...]
where the time goes in v3:
time: 100 us; the launch traced here: 99.9 us
  Pallas kernels  99.3 us (99%)
    pallas_call x1, Pallas kernels, local(): pl.pallas_call(kernel, name='demo_step', out_shape=(pltpu.VMEM((TOK, WIDT...  97.4 us

profile of v3, /device:TPU:1, one launch (start us, length us, event | category | flops | bytes accessed | tf_op | source)
XLA Modules:
  0.0 99.9 jit_solution(929825511250256149)
XLA Ops:
  0.6 97.4 %demo_step.1 = (bf16[384,2048]{1,0:T(8,128)(2,1)S(1)}, bf16[384,2048]{1,0:T(8,128)(2,1)S(1)}, f32[32,2048]{1,0:T(8,128)S(1)}, f32[32,2048]{1,0:T(8,128)S(1)}) custom-call(bf16[384,2048]{1,0:T(8,128)(2,1)} %bitcast.9, bf16[384,2048]{1,0:T(8,128)(2,1)} %bitcast.10, bf16[384,2048]{1,0:T(8,128)(2,1)} %bitcast.11, f32[32,2048]{1,0:T(8,128)} %bitcast.14, ...), custom_call_target="tpu_custom_call" | custom-call | flops 14000000000 | bytes 9000000 | tf_op jit(solution)/shard_map/demo_step/pallas_call | solution.py:506
  98.0 1.9 %place_results.1 = (bf16[384,2048]{1,0:T(8,128)(2,1)}, bf16[384,2048]{1,0:T(8,128)(2,1)}, f32[32,2048]{1,0:T(8,128)}, f32[32,2048]{1,0:T(8,128)}) custom-call(bf16[384,2048]{1,0:T(8,128)(2,1)S(1)} %get-tuple-element.12.refs_0_, bf16[384,2048]{1,0:T(8,128)(2,1)S(1)} %get-tuple-element.13.refs_1_, f32[32,2048]{1,0:T(8,128)S(1)} %get-tuple-element.14.refs_2_, ...), custom_call_target="tpu_custom_call" | custom-call | tf_op jit(solution)/shard_map/place_results/pallas_call | solution.py:526

commit v4 on v3

--- a/solution.py
+++ b/solution.py
@@ -38,11 +38,10 @@
 def kernel(
     head_hbm, gate_hbm, cot_hbm, mom_hbm, idx_hbm, w_hbm, gain_ref, dct_ref, idct_ref,
     hgrad, ggrad, newmom, update,
-    heads, gates, cot, mom, idx, w6, gsend, gt, cslot, p2s, p2r, q, p3s, p3r, dec, dec_r, pair, pair_r,
-    spread,
+    heads, gates, cot, mom, idx, w6, gsend, gt, cslot, p2s, p2r, q, p3s, p3r, dec, dec_r, chosen,
     load_sem, own_sem,
-    wx_s, wx_r, wy_s, wy_r, up_s, up_r, dn_s, dn_r, sib_s, sib_r,
-    c1_s, c1_r, c2_s, c2_r, gt_s, gt_r, s2_s, s2_r, s3_s, s3_r, d_s, d_r, e_s, e_r,
+    w1_s, w1_r, w2_s, w2_r, up_s, up_r, dn_s, dn_r, sib_s, sib_r,
+    c1_s, c1_r, c2_s, c2_r, gt_s, gt_r, s2_s, s2_r, s3_s, s3_r, d_s, d_r,
 ):
     f = lax.axis_index("fsdp")
     g = lax.axis_index("group")
@@ -50,6 +49,7 @@
     lo, core = g // 2, g % 2
     sibling = {"fsdp": f, "group": g + 1 - 2 * core}
     across = {"fsdp": f, "group": (g + 2) % 4}
+    diagonal = {"fsdp": f, "group": 3 - g}
     above = {"fsdp": y * 16 + ((z + lo) % 4) * 4 + x, "group": (g + 2) % 4}
     below = {"fsdp": y * 16 + ((z + 3 + lo) % 4) * 4 + x, "group": (g + 2) % 4}
 
@@ -65,35 +65,38 @@
     along = (at_x, at_y)
     mine = (x, y)
 
-    barrier = pltpu.get_barrier_semaphore()
-    partners = [at(d) for at in (at_x, at_y, at_z) for d in (1, 2, 3)] + [sibling, above, below]
-    for device in partners:
-        pl.semaphore_signal(barrier, inc=1, device_id=device, device_id_type=MESH)
-    pl.semaphore_wait(barrier, len(partners))
-
-    def wx(d):
+    outer = (1 - core) * y + core * x
+    inner = (1 - core) * x + core * y
+
+    def at_inner(d):
+        return {"fsdp": (1 - core) * at_x(d)["fsdp"] + core * at_y(d)["fsdp"], "group": g}
+
+    def at_outer(d):
+        return {"fsdp": (1 - core) * at_y(d)["fsdp"] + core * at_x(d)["fsdp"], "group": g}
+
+    def w1(d):
         half = w_hbm.at[pl.ds(pl.multiple_of(core * 16, 16), 16)]
-        return remote(half, w6.at[y, z, x, core], wx_s.at[d - 1], wx_r.at[d - 1], at_x(d))
-
-    def wy(d):
-        part = w6.at[y, z, :, core]
-        return remote(part, part, wy_s.at[d - 1], wy_r.at[d - 1], at_y(d))
+        return remote(half, w6.at[outer, z, inner, core], w1_s.at[d - 1], w1_r.at[d - 1], at_inner(d))
+
+    def w2(d):
+        part = w6.at[outer, z, :, core]
+        return remote(part, part, w2_s.at[d - 1], w2_r.at[d - 1], at_outer(d))
 
     def up(p):
-        part = w6.at[(y + UP_ORDER[p]) % 4, (z + 8 - p // 4 - 1 + lo) % 4, :, core]
+        part = w6.at[(outer + UP_ORDER[p]) % 4, (z + 8 - p // 4 - 1 + lo) % 4, :, core]
         return remote(part, part, up_s.at[p], up_r.at[p], above)
 
     def down(p):
-        part = w6.at[(y + DOWN_ORDER[p]) % 4, (z + p // 4 + lo) % 4, :, core]
+        part = w6.at[(outer + DOWN_ORDER[p]) % 4, (z + p // 4 + lo) % 4, :, core]
         return remote(part, part, dn_s.at[p], dn_r.at[p], below)
 
     def to_sibling(n):
         if n < 4:
-            part = w6.at[(y + n) % 4, z, :, core]
+            part = w6.at[(outer + n) % 4, z, :, core]
         elif n < 10:
-            part = w6.at[(y + UP_ORDER[n - 4]) % 4, (z + 3 - (n - 4) // 4) % 4, :, core]
+            part = w6.at[(outer + UP_ORDER[n - 4]) % 4, (z + 3 - (n - 4) // 4) % 4, :, core]
         else:
-            part = w6.at[(y + DOWN_ORDER[n - 10]) % 4, (z + 1 + (n - 10) // 4) % 4, :, core]
+            part = w6.at[(outer + DOWN_ORDER[n - 10]) % 4, (z + 1 + (n - 10) // 4) % 4, :, core]
         return remote(part, part, sib_s.at[n], sib_r.at[n], sibling)
 
     def first(axis, s, way, half):
@@ -125,17 +128,15 @@
     def stage3(n, d):
         return remote(p3s.at[n, d - 1], p3r.at[n, d - 1], s3_s.at[n, d - 1], s3_r.at[n, d - 1], at_z(d))
 
-    def to_pair(n):
-        return remote(dec.at[n], dec_r.at[n], d_s.at[n], d_r.at[n], sibling)
-
-    def to_across(n):
-        return remote(pair.at[n], pair_r.at[n], e_s.at[n], e_r.at[n], across)
+    def exchange(n, way):
+        device = (diagonal, across, sibling)[way]
+        return remote(dec.at[n], dec_r.at[n, way], d_s.at[n, way], d_r.at[n, way], device)
 
     loads = [
         pltpu.make_async_copy(head_hbm, heads, load_sem.at[0]),
         pltpu.make_async_copy(gate_hbm, gates, load_sem.at[1]),
         pltpu.make_async_copy(
-            w_hbm.at[pl.ds(pl.multiple_of(core * 16, 16), 16)], w6.at[y, z, x, core], load_sem.at[2]
+            w_hbm.at[pl.ds(pl.multiple_of(core * 16, 16), 16)], w6.at[outer, z, inner, core], load_sem.at[2]
         ),
     ]
     for axis in range(2):
@@ -152,22 +153,20 @@
         pltpu.make_async_copy(mom_hbm, mom, load_sem.at[8]),
         pltpu.make_async_copy(idx_hbm, idx, load_sem.at[9]),
     ]
+    for load in loads:
+        load.start()
+
+    barrier = pltpu.get_barrier_semaphore()
+    partners = [at(d) for at in (at_x, at_y, at_z) for d in (1, 2, 3)] + [sibling, diagonal, above, below]
+    for device in partners:
+        pl.semaphore_signal(barrier, inc=1, device_id=device, device_id_type=MESH)
+    pl.semaphore_wait(barrier, len(partners))
+
     for d in (1, 2, 3):
-        wx(d).start()
-    for load in loads[:3]:
-        load.start()
+        w1(d).start()
     for way in range(2):
         first(0, 0, way, way).start()
         first(1, 0, way, way).start()
-    for way in range(2):
-        first(0, 0, way, 1 - way).start()
-    for load in loads[3:]:
-        load.start()
-
-    row = lax.broadcasted_iota(jnp.int32, (SUB, SUB), 0)
-    col = lax.broadcasted_iota(jnp.int32, (SUB, SUB), 1)
-    quarter, block = row >> 7, (row >> 4) & 7
-    spread[...] = jnp.where((block == (col >> 6)) & (quarter == ((col >> 4) & 3)), 1.0, 0.0).astype(BF16)
 
     gain = gain_ref[...]
     loads[0].wait()
@@ -192,12 +191,9 @@
     for load in loads[2:]:
         load.wait()
     for d in (1, 2, 3):
-        wx(d).wait_recv()
+        w1(d).wait_recv()
     for d in (1, 3, 2):
-        wy(d).start()
-    for way in range(2):
-        first(1, 0, way, 1 - way).start()
-
+        w2(d).start()
     @pl.when(lo == 1)
     def _():
         up(0).start()
@@ -209,9 +205,6 @@
     to_sibling(0).start()
 
     lax.fori_loop(1, 4, gated_block, 0)
-    for d in (2, 1, 3):
-        for axis in range(2):
-            gated_to(axis, d).start()
     for axis in range(2):
         own_gated(axis).start()
 
@@ -295,6 +288,27 @@
         for d in (1, 2, 3):
             gated_to(axis, d).wait_recv()
 
+    def stacked(v):
+        return jnp.concatenate([v[:, k * 128 : (k + 1) * 128] for k in range(4)], axis=0)
+
+    def choose():
+        row = lax.broadcasted_iota(jnp.int32, (SUB, SUB), 0)
+        col = lax.broadcasted_iota(jnp.int32, (SUB, SUB), 1)
+        same = (((row >> 4) & 7) == (col >> 6)) & ((row >> 7) == ((col >> 4) & 3))
+        spread = jnp.where(same, 1.0, 0.0).astype(BF16)
+        where = stacked(idx[...])
+        bits = jnp.left_shift(jnp.ones_like(where), where & 15)
+        bits = jnp.concatenate(
+            [jnp.where((where >> 4) == k, bits, 0).astype(F32).astype(BF16) for k in range(4)], axis=1
+        )
+        words = jnp.dot(bits, spread, preferred_element_type=F32).astype(jnp.int32)
+        lane = lax.broadcasted_iota(jnp.int32, (4 * ROWS, SUB), 1)
+        kept = (lax.shift_right_logical(words, lane & 15) & 1).astype(F32)
+        for n in range(4):
+            axis, s = PIECES[n]
+            piece = axis * 2 + s
+            chosen[n] = stacked(kept[piece * ROWS : (piece + 1) * ROWS])
+
     def moment_step(n):
         axis, s = PIECES[n]
         start = (axis * 2 + s) * SUB
@@ -303,46 +317,31 @@
         own = q[n, pl.ds(pl.multiple_of(z * ROWS, ROWS), ROWS), :]
         gradient = (own + p3r[n, 0].astype(F32)) + (p3r[n, 1].astype(F32) + p3r[n, 2].astype(F32))
         moment = DECAY * mom[:, start : start + SUB] + gradient * ((TOK * 64) ** -0.5)
-        where = idx[:, start // 4 : start // 4 + 128]
-        bits = jnp.left_shift(jnp.ones_like(where), where & 15)
-        bits = jnp.concatenate(
-            [jnp.where((where >> 4) == k, bits, 0).astype(F32).astype(BF16) for k in range(4)], axis=1
-        )
-        words = jnp.dot(bits, spread[...], preferred_element_type=F32).astype(jnp.int32)
-        lane = lax.broadcasted_iota(jnp.int32, (ROWS, SUB), 1)
-        chosen = (lax.shift_right_logical(words, lane & 15) & 1).astype(F32)
-
-        def stacked(v):
-            return jnp.concatenate([v[:, k * 128 : (k + 1) * 128] for k in range(4)], axis=0)
-
         coeffs = jnp.dot(stacked(moment), dct_ref[...], precision=HIGHEST, preferred_element_type=F32)
         decoded = jnp.dot(
-            coeffs * stacked(chosen), idct_ref[...], precision=HIGHEST, preferred_element_type=F32
+            coeffs * chosen[n], idct_ref[...], precision=HIGHEST, preferred_element_type=F32
         )
         decoded = jnp.concatenate([decoded[k * ROWS : (k + 1) * ROWS] for k in range(4)], axis=1)
         dec[n] = decoded
-        to_pair(n).start()
+        for way in range(3):
+            exchange(n, way).start()
         newmom[:, start : start + SUB] = moment - decoded
-
-    def pair_step(n):
-        to_pair(n).wait_recv()
-        pair[n] = dec[n] + dec_r[n]
-        to_across(n).start()
 
     def update_step(n):
         axis, s = PIECES[n]
-        to_across(n).wait_recv()
         start = (axis * 2 + s) * SUB
-        update[:, start : start + SUB] = (pair[n] + pair_r[n]) * 0.25
-
-    def back(block, pieces, arrivals):
-        for n in arrivals:
-            to_sibling(n).wait_recv()
-        ys = [(y + j) % 4 for j in pieces]
-
-        weight = jnp.concatenate([w6[v, block].reshape(HDIM, WIDTH) for v in ys], axis=0)
+        for way in range(3):
+            exchange(n, way).wait_recv()
+        update[:, start : start + SUB] = ((dec[n] + dec_r[n, 2]) + (dec_r[n, 0] + dec_r[n, 1])) * 0.25
+
+    def back(block, ys):
+        halves = []
+        for v in ys:
+            for k in range(4):
+                halves += [w6[v, block, k, 0], w6[k, block, v, 1]]
+        weight = jnp.concatenate(halves, axis=0)
         both = lax.dot_general(cot[...], weight, (((1,), (1,)), ((), ())), preferred_element_type=F32)
-        for part in range(2):
+        for part in range(len(ys)):
             head = ys[part] * 4 + block
             cols = pl.ds(pl.multiple_of(head * HDIM, HDIM), HDIM)
             u = both[:, part * HDIM : (part + 1) * HDIM]
@@ -357,71 +356,74 @@
 
     prev, prev2, after = (z + 3) % 4, (z + 2) % 4, (z + 1) % 4
 
-    relay(0)
+    def block_back(block, arrivals):
+        for n in arrivals:
+            to_sibling(n).wait_recv()
+        back(block, (0, 1))
+        back(block, (2, 3))
+
+    for way in range(2):
+        first(0, 0, way, 1 - way).start()
+        first(1, 0, way, 1 - way).start()
+    for d in (2, 1, 3):
+        for axis in range(2):
+            gated_to(axis, d).start()
     for j in (1, 3):
-        wy(4 - j).wait_recv()
+        w2(4 - j).wait_recv()
         own_piece(j)
+    w2(2).wait_recv()
+    own_piece(2)
     pass_second(0, 0)
+    pass_second(1, 0)
     for half in range(2):
         for way in range(2):
             first(0, 1, way, (way + half) % 2).start()
-    wy(2).wait_recv()
-    own_piece(2)
+            first(1, 1, way, (way + half) % 2).start()
+    relay(0)
     follow(0)
-    back(z, (0, 1), (0, 1))
+    choose()
     relay(1)
-    pass_second(1, 0)
-    for half in range(2):
-        for way in range(2):
-            first(1, 1, way, (way + half) % 2).start()
-    back(z, (2, 3), (2, 3))
+    block_back(z, range(4))
     relay(2)
     follow(1)
+    relay(3)
+    follow(2)
+    relay(4)
+    follow(3)
     gated_in(0)
     second_in(0, 0)
     terms(0)
-    relay(3)
-    follow(2)
-    back(prev, (0, 1), (4, 5))
-    relay(4)
-    follow(3)
-    pass_second(0, 1)
     gated_in(1)
     second_in(1, 0)
     terms(1)
     relay(5)
     follow(4)
-    back(after, (2, 3), (11, 13))
+    block_back(prev, range(4, 8))
+    pass_second(0, 1)
     pass_second(1, 1)
+    block_back(after, range(10, 14))
+    follow(5)
+    sum2(0)
+    sum2(1)
     second_in(0, 1)
     terms(2)
-    follow(5)
-    sum2(1)
-    back(prev, (2, 3), (6, 7))
-    sum2(0)
-    back(after, (0, 1), (10, 12))
-    moment_step(1)
     second_in(1, 1)
     terms(3)
     moment_step(0)
-    pair_step(1)
-    back(prev2, (0, 1), (8, 9))
-    pair_step(0)
+    moment_step(1)
+    block_back(prev2, (8, 9, 14, 15))
     sum2(2)
     sum2(3)
     update_step(0)
     update_step(1)
-    back(prev2, (2, 3), (14, 15))
     moment_step(2)
     moment_step(3)
-    pair_step(2)
-    pair_step(3)
     update_step(2)
     update_step(3)
 
     for d in (1, 2, 3):
-        wx(d).wait_send()
-        wy(d).wait_send()
+        w1(d).wait_send()
+        w2(d).wait_send()
         for axis in range(2):
             gated_to(axis, d).wait_send()
         for n in range(4):
@@ -439,8 +441,8 @@
                 first(axis, s, way, 1).wait_send()
                 second(axis, s, way).wait_send()
     for n in range(4):
-        to_pair(n).wait_send()
-        to_across(n).wait_send()
+        for way in range(3):
+            exchange(n, way).wait_send()
 
 
 def place(*refs):
@@ -490,10 +492,8 @@
         pltpu.VMEM((4, 3, ROWS, SUB), BF16),
         pltpu.VMEM((4, 3, ROWS, SUB), BF16),
         pltpu.VMEM((4, ROWS, SUB), F32),
-        pltpu.VMEM((4, ROWS, SUB), F32),
-        pltpu.VMEM((4, ROWS, SUB), F32),
-        pltpu.VMEM((4, ROWS, SUB), F32),
-        pltpu.VMEM((SUB, SUB), BF16),
+        pltpu.VMEM((4, 3, ROWS, SUB), F32),
+        pltpu.VMEM((4, 128, 128), F32),
         dma((10,)), dma((2,)),
         dma((3,)), dma((3,)), dma((3,)), dma((3,)),
         dma((6,)), dma((6,)), dma((6,)), dma((6,)),
@@ -501,7 +501,7 @@
         dma((2, 2, 2, 2)), dma((2, 2, 2, 2)), dma((2, 2, 2)), dma((2, 2, 2)),
         dma((2, 3)), dma((2, 3)),
         dma((4, 3)), dma((4, 3)), dma((4, 3)), dma((4, 3)),
-        dma((4,)), dma((4,)), dma((4,)), dma((4,)),
+        dma((4, 3)), dma((4, 3)),
     ]
     results = pl.pallas_call(
         kernel,

time: 100 us -> 96 us (0.960)
  Pallas kernels: 99.3 us -> 95.3 us
    pallas_call x1, Pallas kernels: 97.4 us -> 93.4 us  [local(): pl.pallas_call(kernel, name='demo_step', out_shape=(pltpu.VMEM((TOK, WIDT...]
where the time goes in v4:
time: 96 us; the launch traced here: 95.9 us
  Pallas kernels  95.3 us (99%)
    pallas_call x1, Pallas kernels, local(): pl.pallas_call(kernel, name='demo_step', out_shape=(pltpu.VMEM((TOK, WIDT...  93.4 us

profile of v4, /device:TPU:1, one launch (start us, length us, event | category | flops | bytes accessed | tf_op | source)
XLA Modules:
  0.0 95.9 jit_solution(10568393988342478925)
XLA Ops:
  0.6 93.4 %demo_step.1 = (bf16[384,2048]{1,0:T(8,128)(2,1)S(1)}, bf16[384,2048]{1,0:T(8,128)(2,1)S(1)}, f32[32,2048]{1,0:T(8,128)S(1)}, f32[32,2048]{1,0:T(8,128)S(1)}) custom-call(bf16[384,2048]{1,0:T(8,128)(2,1)} %bitcast.9, bf16[384,2048]{1,0:T(8,128)(2,1)} %bitcast.10, bf16[384,2048]{1,0:T(8,128)(2,1)} %bitcast.11, f32[32,2048]{1,0:T(8,128)} %bitcast.14, ...), custom_call_target="tpu_custom_call" | custom-call | flops 14000000000 | bytes 9000000 | tf_op jit(solution)/shard_map/demo_step/pallas_call | solution.py:506
  94.0 1.9 %place_results.1 = (bf16[384,2048]{1,0:T(8,128)(2,1)}, bf16[384,2048]{1,0:T(8,128)(2,1)}, f32[32,2048]{1,0:T(8,128)}, f32[32,2048]{1,0:T(8,128)}) custom-call(bf16[384,2048]{1,0:T(8,128)(2,1)S(1)} %get-tuple-element.12.refs_0_, bf16[384,2048]{1,0:T(8,128)(2,1)S(1)} %get-tuple-element.13.refs_1_, f32[32,2048]{1,0:T(8,128)S(1)} %get-tuple-element.14.refs_2_, ...), custom_call_target="tpu_custom_call" | custom-call | tf_op jit(solution)/shard_map/place_results/pallas_call | solution.py:526

commit v5 on v4

--- a/solution.py
+++ b/solution.py
@@ -365,9 +365,10 @@
     for way in range(2):
         first(0, 0, way, 1 - way).start()
         first(1, 0, way, 1 - way).start()
-    for d in (2, 1, 3):
+    for d in (1, 3, 2):
         for axis in range(2):
             gated_to(axis, d).start()
+    choose()
     for j in (1, 3):
         w2(4 - j).wait_recv()
         own_piece(j)
@@ -381,7 +382,6 @@
             first(1, 1, way, (way + half) % 2).start()
     relay(0)
     follow(0)
-    choose()
     relay(1)
     block_back(z, range(4))
     relay(2)
@@ -396,11 +396,11 @@
     gated_in(1)
     second_in(1, 0)
     terms(1)
+    pass_second(0, 1)
+    pass_second(1, 1)
     relay(5)
     follow(4)
     block_back(prev, range(4, 8))
-    pass_second(0, 1)
-    pass_second(1, 1)
     block_back(after, range(10, 14))
     follow(5)
     sum2(0)

time: 96 us -> 94.8 us (0.987)
  Pallas kernels: 95.3 us -> 93.7 us
    pallas_call x1, Pallas kernels: 93.4 us -> 91.8 us  [local(): pl.pallas_call(kernel, name='demo_step', out_shape=(pltpu.VMEM((TOK, WIDT...]
where the time goes in v5:
time: 94.8 us; the launch traced here: 94.3 us
  Pallas kernels  93.7 us (99%)
    pallas_call x1, Pallas kernels, local(): pl.pallas_call(kernel, name='demo_step', out_shape=(pltpu.VMEM((TOK, WIDT...  91.8 us

profile of v5, /device:TPU:1, one launch (start us, length us, event | category | flops | bytes accessed | tf_op | source)
XLA Modules:
  0.0 94.3 jit_solution(4543030347944736734)
XLA Ops:
  0.6 91.8 %demo_step.1 = (bf16[384,2048]{1,0:T(8,128)(2,1)S(1)}, bf16[384,2048]{1,0:T(8,128)(2,1)S(1)}, f32[32,2048]{1,0:T(8,128)S(1)}, f32[32,2048]{1,0:T(8,128)S(1)}) custom-call(bf16[384,2048]{1,0:T(8,128)(2,1)} %bitcast.9, bf16[384,2048]{1,0:T(8,128)(2,1)} %bitcast.10, bf16[384,2048]{1,0:T(8,128)(2,1)} %bitcast.11, f32[32,2048]{1,0:T(8,128)} %bitcast.14, ...), custom_call_target="tpu_custom_call" | custom-call | flops 14000000000 | bytes 9000000 | tf_op jit(solution)/shard_map/demo_step/pallas_call | solution.py:506
  92.4 1.9 %place_results.1 = (bf16[384,2048]{1,0:T(8,128)(2,1)}, bf16[384,2048]{1,0:T(8,128)(2,1)}, f32[32,2048]{1,0:T(8,128)}, f32[32,2048]{1,0:T(8,128)}) custom-call(bf16[384,2048]{1,0:T(8,128)(2,1)S(1)} %get-tuple-element.12.refs_0_, bf16[384,2048]{1,0:T(8,128)(2,1)S(1)} %get-tuple-element.13.refs_1_, f32[32,2048]{1,0:T(8,128)S(1)} %get-tuple-element.14.refs_2_, ...), custom_call_target="tpu_custom_call" | custom-call | tf_op jit(solution)/shard_map/place_results/pallas_call | solution.py:526

commit v6 on v5

--- a/solution.py
+++ b/solution.py
@@ -36,9 +36,9 @@
 
 
 def kernel(
-    head_hbm, gate_hbm, cot_hbm, mom_hbm, idx_hbm, w_hbm, gain_ref, dct_ref, idct_ref,
+    head_hbm, gate_hbm, cot_hbm, mom_hbm, idx_hbm, w_hbm, gain_hbm, dct_hbm, idct_hbm,
     hgrad, ggrad, newmom, update,
-    heads, gates, cot, mom, idx, w6, gsend, gt, cslot, p2s, p2r, q, p3s, p3r, dec, dec_r, chosen,
+    heads, gates, cot, mom, idx, w6, gsend, gt, cslot, p2s, p2r, q, p3s, p3r, dec, dec_r, chosen, gain_ref, dct_ref, idct_ref,
     load_sem, own_sem,
     w1_s, w1_r, w2_s, w2_r, up_s, up_r, dn_s, dn_r, sib_s, sib_r,
     c1_s, c1_r, c2_s, c2_r, gt_s, gt_r, s2_s, s2_r, s3_s, s3_r, d_s, d_r,
@@ -152,7 +152,11 @@
         pltpu.make_async_copy(cot_hbm, cot, load_sem.at[7]),
         pltpu.make_async_copy(mom_hbm, mom, load_sem.at[8]),
         pltpu.make_async_copy(idx_hbm, idx, load_sem.at[9]),
+        pltpu.make_async_copy(dct_hbm, dct_ref, load_sem.at[10]),
+        pltpu.make_async_copy(idct_hbm, idct_ref, load_sem.at[11]),
     ]
+    gain_load = pltpu.make_async_copy(gain_hbm, gain_ref, load_sem.at[12])
+    gain_load.start()
     for load in loads:
         load.start()
 
@@ -168,6 +172,7 @@
         first(0, 0, way, way).start()
         first(1, 0, way, way).start()
 
+    gain_load.wait()
     gain = gain_ref[...]
     loads[0].wait()
     loads[1].wait()
@@ -494,7 +499,10 @@
         pltpu.VMEM((4, ROWS, SUB), F32),
         pltpu.VMEM((4, 3, ROWS, SUB), F32),
         pltpu.VMEM((4, 128, 128), F32),
-        dma((10,)), dma((2,)),
+        pltpu.VMEM((1, HDIM), F32),
+        pltpu.VMEM((128, 128), F32),
+        pltpu.VMEM((128, 128), F32),
+        dma((13,)), dma((2,)),
         dma((3,)), dma((3,)), dma((3,)), dma((3,)),
         dma((6,)), dma((6,)), dma((6,)), dma((6,)),
         dma((16,)), dma((16,)),
@@ -512,7 +520,7 @@
             pltpu.VMEM((ROWS, WIDTH), F32),
             pltpu.VMEM((ROWS, WIDTH), F32),
         ),
-        in_specs=[anywhere] * 6 + [vmem] * 3,
+        in_specs=[anywhere] * 9,
         out_specs=(vmem,) * 4,
         scratch_shapes=scratch,
         compiler_params=pltpu.CompilerParams(

time: 94.8 us -> 94 us (level)
  no operation moved by 1% of the time
where the time goes in v6:
time: 94 us; the launch traced here: 93.6 us
  Pallas kernels  93 us (99%)
    pallas_call x1, Pallas kernels, local(): pl.pallas_call(kernel, name='demo_step', out_shape=(pltpu.VMEM((TOK, WIDT...  91.1 us
    pallas_call x1, Pallas kernels, local(): pl.pallas_call(place, name='place_results', out_shape=tuple((jax.ShapeDty...  1.89 us

profile of v6, /device:TPU:1, one launch (start us, length us, event | category | flops | bytes accessed | tf_op | source)
XLA Modules:
  0.0 93.6 jit_solution(12450522263970388066)
XLA Ops:
  0.6 91.1 %demo_step.1 = (bf16[384,2048]{1,0:T(8,128)(2,1)S(1)}, bf16[384,2048]{1,0:T(8,128)(2,1)S(1)}, f32[32,2048]{1,0:T(8,128)S(1)}, f32[32,2048]{1,0:T(8,128)S(1)}) custom-call(bf16[384,2048]{1,0:T(8,128)(2,1)} %bitcast.9, bf16[384,2048]{1,0:T(8,128)(2,1)} %bitcast.10, bf16[384,2048]{1,0:T(8,128)(2,1)} %bitcast.11, f32[32,2048]{1,0:T(8,128)} %bitcast.14, ...), custom_call_target="tpu_custom_call" | custom-call | flops 14000000000 | bytes 9000000 | tf_op jit(solution)/shard_map/demo_step/pallas_call | solution.py:514
  91.7 1.9 %place_results.1 = (bf16[384,2048]{1,0:T(8,128)(2,1)}, bf16[384,2048]{1,0:T(8,128)(2,1)}, f32[32,2048]{1,0:T(8,128)}, f32[32,2048]{1,0:T(8,128)}) custom-call(bf16[384,2048]{1,0:T(8,128)(2,1)S(1)} %get-tuple-element.12.refs_0_, bf16[384,2048]{1,0:T(8,128)(2,1)S(1)} %get-tuple-element.13.refs_1_, f32[32,2048]{1,0:T(8,128)S(1)} %get-tuple-element.14.refs_2_, ...), custom_call_target="tpu_custom_call" | custom-call | tf_op jit(solution)/shard_map/place_results/pallas_call | solution.py:534
